TPU v7x, 32 devices: a whole 2x2x4 slice. The times are simulated.
32 devices in a mesh: pipe: 2 (over y), expert: 16 (over z, x, core).
Axes of the slice: x: 2, y: 2, z: 4, core: 2. Of those that a mesh axis runs over, the one named last changes fastest.
Arguments:
- tokens: bfloat16 [4096, 2048], P(('pipe', 'expert')), may hold values from -6 to 6
- cotangent: bfloat16 [4096, 2048], P(('pipe', 'expert')), may hold values from -6 to 6
- expert_ids: int32 [4096, 8], P(('pipe', 'expert')), may hold values from 0 to 127, all different within a row
- gates: float32 [4096, 8], P(('pipe', 'expert')), may hold values from 0.05 to 0.5
- w_gate: bfloat16 [2, 2048, 3072], P('pipe', None, 'expert'), as said below
- w_up: bfloat16 [2, 2048, 3072], P('pipe', None, 'expert'), as said below
- w_down: bfloat16 [2, 3072, 2048], P('pipe', 'expert'), as said below
Outputs:
- mixed_out: bfloat16 [4096, 2048], P(('pipe', 'expert'))
- token_grad: bfloat16 [4096, 2048], P(('pipe', 'expert'))
- gate_grad: float32 [4096, 8], P(('pipe', 'expert'))
- down_grad: bfloat16 [2, 3072, 1024], P('pipe', 'expert')
Inputs may be any that keep to these rules, and one draw needn't show every extreme that they name: `expert_ids`: each row names 8 different experts. `w_gate`: the blocks of pipe index p and 1 - p are equal. `w_up`: the blocks of pipe index p and 1 - p are equal. `w_down`: the blocks of pipe index p and 1 - p are equal.
All inputs are finite; a program needn't handle non-finite values.
Results may differ from a plain program's by a relative error of at most 0.0065.
Values may be sent and summed in bfloat16 or wider, within the bound.
A program may use at most 64 MiB of HBM per device.

v0:
```python
import jax
import jax.numpy as jnp
from jax import lax
from jax.sharding import PartitionSpec as P

WS = 4


def from_partner(block, axis, stride):
    count = lax.axis_size(axis)
    route = []
    for low in range(count):
        high = low | 1 << stride
        if high != low and high < count:
            route += [(low, high), (high, low)]
    return lax.ppermute(block, axis, route)


def silu_parts(preact):
    sigmoid_val = jax.nn.sigmoid(preact)
    return (preact * sigmoid_val, sigmoid_val * (1.0 + preact * (1.0 - sigmoid_val)))


def expert_rows(inputs, scaled, gate_cols, up_cols, down_rows):
    transposed = (((1,), (1,)), ((), ()))
    gate_pre = jnp.dot(inputs, gate_cols, preferred_element_type=jnp.float32)
    up_pre = jnp.dot(inputs, up_cols, preferred_element_type=jnp.float32)
    activated, slope_val = silu_parts(gate_pre)
    hidden = (activated * up_pre).astype(jnp.bfloat16)
    group_out = jnp.dot(hidden, down_rows, preferred_element_type=jnp.float32).astype(jnp.bfloat16)
    hidden_grad = lax.dot_general(scaled, down_rows, transposed, preferred_element_type=jnp.float32)
    grad_gate = (hidden_grad * up_pre * slope_val).astype(jnp.bfloat16)
    grad_up = (hidden_grad * activated).astype(jnp.bfloat16)
    back_gate = lax.dot_general(
        grad_gate, gate_cols, transposed, preferred_element_type=jnp.float32
    )
    back_up = lax.dot_general(grad_up, up_cols, transposed, preferred_element_type=jnp.float32)
    group_grad = (back_gate + back_up).astype(jnp.bfloat16)
    return (hidden, group_out, group_grad)


def split_half(stacked, upper_half):
    half_width = stacked.shape[-1] // 2
    lower_part = stacked[..., :half_width]
    upper_part = stacked[..., half_width:]
    kept_half = jnp.where(upper_half, upper_part, lower_part)
    sent_half = jnp.where(upper_half, lower_part, upper_part)
    return (kept_half, sent_half)


def body(tokens, cotangent, expert_ids, gates, w_gate, w_up, w_down):
    highest = lax.Precision.HIGHEST
    tok_count, model_width = tokens.shape
    chosen_count = expert_ids.shape[1]
    devices = lax.axis_size("expert")
    shards = WS
    experts_here = devices // shards
    capacity = tok_count // 24
    slot_count = experts_here * capacity
    flat_ids = expert_ids.reshape(-1)
    window_ids = jnp.arange(experts_here, dtype=jnp.int32)
    onehot = (flat_ids[:, None] == window_ids[None, :]).astype(jnp.int32)
    earlier = jnp.cumsum(onehot, axis=0) - onehot
    slot_rank = jnp.sum(earlier * onehot, axis=1)
    in_window = (flat_ids < experts_here) & (slot_rank < capacity)
    target_slot = jnp.where(in_window, flat_ids * capacity + slot_rank, slot_count)
    slot_numbers = jnp.arange(slot_count, dtype=jnp.int32)
    pick_pair = (target_slot[None, :] == slot_numbers[:, None]).astype(jnp.float32)
    pick_token = pick_pair.reshape(slot_count, tok_count, chosen_count).sum(axis=2)
    slot_gate = jnp.dot(pick_pair, gates.reshape(-1), precision=highest)
    pick_narrow = pick_token.astype(jnp.bfloat16)
    slot_rows = jnp.dot(pick_narrow, tokens, preferred_element_type=jnp.float32).astype(
        jnp.bfloat16
    )
    slot_cot = jnp.dot(pick_narrow, cotangent, preferred_element_type=jnp.float32)
    slot_scaled = (slot_gate[:, None] * slot_cot).astype(jnp.bfloat16)

    def spread(rows):
        shaped = rows.reshape(experts_here, 1, capacity, model_width)
        return jnp.broadcast_to(shaped, (experts_here, shards, capacity, model_width)).reshape(
            devices, capacity, model_width
        )

    gate_cols = w_gate[0]
    up_cols = w_up[0]
    down_rows = w_down[0]
    inputs = lax.all_to_all(spread(slot_rows), "expert", split_axis=0, concat_axis=0, tiled=True)
    scaled = lax.all_to_all(spread(slot_scaled), "expert", split_axis=0, concat_axis=0, tiled=True)
    sources, item_count, _ = inputs.shape
    hidden, group_out, group_grad = expert_rows(
        inputs.reshape(-1, model_width),
        scaled.reshape(-1, model_width),
        gate_cols,
        up_cols,
        down_rows,
    )
    hidden = hidden.reshape(sources, item_count, -1)
    stacked = jnp.stack(
        [
            group_out.reshape(sources, item_count, model_width),
            group_grad.reshape(sources, item_count, model_width),
        ]
    )
    back_out = lax.all_to_all(stacked[0], "expert", split_axis=0, concat_axis=0, tiled=True)
    back_grad = lax.all_to_all(stacked[1], "expert", split_axis=0, concat_axis=0, tiled=True)
    back_out, back_grad, hidden, scaled = (back_out, back_grad, hidden, scaled)
    expert_out = (
        back_out.reshape(experts_here, shards, capacity, model_width)
        .astype(jnp.float32)
        .sum(axis=1)
        .reshape(slot_count, model_width)
    )
    grad_terms = (
        back_grad.reshape(experts_here, shards, capacity, model_width)
        .astype(jnp.float32)
        .sum(axis=1)
        .reshape(slot_count, model_width)
    )
    weighted = slot_gate[:, None] * expert_out
    mixed_out = jnp.dot(pick_token.T, weighted, precision=highest).astype(jnp.bfloat16)
    slot_value = jnp.sum(slot_cot * expert_out, axis=1)
    gate_grad = jnp.dot(slot_value, pick_pair, precision=highest).reshape(tok_count, chosen_count)
    token_grad = jnp.dot(pick_token.T, grad_terms, precision=highest).astype(jnp.bfloat16)
    local_down = lax.dot_general(
        hidden.reshape(-1, hidden.shape[-1]),
        scaled.reshape(-1, model_width),
        (((0,), (0,)), ((), ())),
        preferred_element_type=jnp.float32,
    ).astype(jnp.bfloat16)
    sections = lax.axis_size("pipe")
    section_pos = lax.axis_index("pipe")
    kept_half, sent_half = split_half(local_down, section_pos >= sections // 2)
    travelled = sent_half
    for bit_pos in range(sections.bit_length() - 1):
        travelled = from_partner(travelled, "pipe", bit_pos)
    partner_part = travelled.astype(jnp.float32)
    down_grad = (kept_half.astype(jnp.float32) + partner_part).astype(jnp.bfloat16)[None]
    return (mixed_out, token_grad, gate_grad, down_grad)


def solution(mesh):
    placed = (
        P(("pipe", "expert"), None),
        P(("pipe", "expert"), None),
        P(("pipe", "expert"), None),
        P(("pipe", "expert"), None),
        P("pipe", None, "expert"),
        P("pipe", None, "expert"),
        P("pipe", "expert", None),
    )
    return jax.shard_map(
        body,
        mesh=mesh,
        in_specs=placed,
        out_specs=(
            P(("pipe", "expert"), None),
            P(("pipe", "expert"), None),
            P(("pipe", "expert"), None),
            P("pipe", "expert", None),
        ),
        check_vma=False,
    )
```

profile of v0, /device:TPU:0, one launch (start us, length us, event | category | flops | bytes accessed | tf_op | source)
XLA Modules:
  0.0 97.1 jit_solution(4523105164650640612)
XLA Ops:
  0.6 0.9 copy.28
  1.7 1.1 %reduce-window.6 = s32[4,8,128]{2,1,0:T(8,128)S(1)} reduce-window(s32[4,8,128]{2,1,0:T(8,128)S(1)} %fusion.21, s32[]{:T(128)} %constant.5.clone.1), window={size=1x1x128 pad=0_0x0_0x127_0}, to_apply=%region_0.0 | reduce-window | flops 520192 | bytes 32772 | tf_op jit(solution)/shard_map/reduce-window
  3.5 0.7 add_select_fusion.1
  4.3 1.2 %convolution_convert_fusion.4 = bf16[20,2048]{1,0:T(8,128)(2,1)S(1)} fusion(bf16[128,2048]{1,0:T(8,128)(2,1)} %param.7, f32[20,128]{1,0:T(8,128)S(1)} %convert_reduce_fusion.2), kind=kOutput, calls=%fused_computation.6 | convolution fusion | flops 10529280 | bytes 616448 | tf_op jit(solution)/shard_map/dot_general | solution.py:72
  5.6 21.8 %all_to_all.20 = bf16[16,5,2048]{2,1,0:T(8,128)(2,1)S(1)} all-to-all(bf16[16,5,2048]{2,1,0:T(8,128)(2,1)S(1)} %bitcast.64), channel_id=1, replica_groups=mesh['pipe'=2,'expert'=16] {'expert'}, dimensions={0} | all-to-all | bytes 655360 | tf_op jit(solution)/shard_map/all_to_all | solution.py:87
  27.5 0.4 fusion.9
  27.9 1.0 %multiply_convert_fusion.3 = (bf16[80,192]{1,0:T(8,128)(2,1)S(1)}, f32[80,192]{1,0:T(8,128)}) fusion(f32[80,192]{1,0:T(8,128)S(1)} %fusion.9, bf16[80,2048]{1,0:T(8,128)(2,1)S(1)} %reshape.95, bf16[1,2048,192]{1,2,0:T(8,128)(2,1)S(1)} %copy-done), kind=kOutput, calls=%fused_computation.33 | convolution fusion | flops 63006720 | bytes 1267712 | tf_op jit(solution)/shard_map/dot_general | solution.py:27
  28.9 0.6 copy-done.5
  29.6 0.3 convolution_convert_fusion.3
  29.8 0.9 squeeze_stack_reshape.6
  30.8 4.1 %all-to-all-start.1 = ((bf16[16,5,2048]{2,1,0:T(8,128)(2,1)}), bf16[16,5,2048]{2,1,0:T(8,128)(2,1)S(1)}, u32[]{:S(2)}, u32[]{:S(2)}) async-start(bf16[16,5,2048]{2,1,0:T(8,128)(2,1)} %squeeze_stack_reshape.6), calls=%async_computation.1 | async-start | bytes 1048576 | tf_op jit(solution)/shard_map/all_to_all | solution.py:104
  35.2 14.1 %all-to-all-done.1 = bf16[16,5,2048]{2,1,0:T(8,128)(2,1)S(1)} async-done(((bf16[16,5,2048]{2,1,0:T(8,128)(2,1)}), bf16[16,5,2048]{2,1,0:T(8,128)(2,1)S(1)}, u32[]{:S(2)}, u32[]{:S(2)}) %all-to-all-start.1) | async-done | bytes 327712 | tf_op jit(solution)/shard_map/all_to_all | solution.py:104
  49.5 1.9 %multiply_reduce_fusion = (f32[20]{0:T(128)}, bf16[20,2048]{1,0:T(8,128)(2,1)S(1)}) fusion(f32[20,2048]{1,0:T(8,128)S(1)} %reshape.96, f32[20]{0:T(128)S(1)} %convolution_bitcast_fusion, bf16[128,2048]{1,0:T(8,128)(2,1)} %param.8, f32[20,128]{1,0:T(8,128)S(1)} %convert_reduce_fusion.2), kind=kOutput, calls=%fused_computation.26 | convolution fusion | flops 10652140 | bytes 780448 | tf_op jit(solution)/shard_map/dot_general | solution.py:75
  51.5 0.8 broadcast_in_dim.33
  52.3 4.1 %all-to-all-start.2 = ((bf16[16,5,2048]{2,1,0:T(8,128)(2,1)}), bf16[16,5,2048]{2,1,0:T(8,128)(2,1)S(1)}, u32[]{:S(2)}, u32[]{:S(2)}) async-start(bf16[16,5,2048]{2,1,0:T(8,128)(2,1)} %bitcast.8), calls=%async_computation.2 | async-start | bytes 1048576 | tf_op jit(solution)/shard_map/all_to_all | solution.py:88
  56.4 0.7 copy.33
  57.2 13.7 %all-to-all-done.2 = bf16[16,5,2048]{2,1,0:T(8,128)(2,1)S(1)} async-done(((bf16[16,5,2048]{2,1,0:T(8,128)(2,1)}), bf16[16,5,2048]{2,1,0:T(8,128)(2,1)S(1)}, u32[]{:S(2)}, u32[]{:S(2)}) %all-to-all-start.2) | async-done | bytes 327712 | tf_op jit(solution)/shard_map/all_to_all | solution.py:88
  71.0 1.2 %convolution_convert_fusion = bf16[192,2048]{1,0:T(8,128)(2,1)S(1)} fusion(bf16[80,192]{1,0:T(8,128)(2,1)} %copy-done.5, bf16[80,2048]{1,0:T(8,128)(2,1)S(1)} %reshape.98), kind=kOutput, calls=%fused_computation | convolution fusion | flops 63307776 | bytes 1144832 | tf_op jit(solution)/shard_map/dot_general | solution.py:124
  72.2 0.4 fusion.1
  72.6 0.8 broadcast_select_fusion
  73.4 1.5 %collective-permute-start = (bf16[192,1024]{1,0:T(8,128)(2,1)}, bf16[192,1024]{1,0:T(8,128)(2,1)}, u32[]{:S(2)}, u32[]{:S(2)}) collective-permute-start(bf16[192,1024]{1,0:T(8,128)(2,1)} %broadcast_select_fusion), channel_id=1, source_target_pairs={{0,16},{16,0},{1,17},{17,1},{2,18},{18,2},{3,19},{19,3},{4,20},{20... | collective-permute-start | bytes 1179656 | tf_op jit(solution)/shard_map/ppermute | solution.py:16
  74.9 0.3 fusion.7
  75.2 0.3 fusion
  75.5 0.9 squeeze_stack_reshape.7
  76.4 4.2 %all-to-all-start.3 = ((bf16[16,5,2048]{2,1,0:T(8,128)(2,1)}), bf16[16,5,2048]{2,1,0:T(8,128)(2,1)S(1)}, u32[]{:S(2)}, u32[]{:S(2)}) async-start(bf16[16,5,2048]{2,1,0:T(8,128)(2,1)} %squeeze_stack_reshape.7), calls=%async_computation.3 | async-start | bytes 1048576 | tf_op jit(solution)/shard_map/all_to_all | solution.py:105
  80.7 0.4 select_reduce_fusion
  81.0 0.7 copy.38
  81.7 1.8 %convolution_convert_fusion.2 = bf16[128,2048]{1,0:T(8,128)(2,1)} fusion(f32[20,128]{1,0:T(8,128)S(1)} %copy-done.8, f32[20,2048]{1,0:T(8,128)S(1)} %copy-done.4, f32[20]{0:T(128)S(1)} %copy-done.12), kind=kOutput, calls=%fused_computation.2 | convolution fusion | flops 63217664 | bytes 698448 | tf_op jit(solution)/shard_map/dot_general | solution.py:120
  83.5 1.2 %collective-permute-done = bf16[192,1024]{1,0:T(8,128)(2,1)} collective-permute-done((bf16[192,1024]{1,0:T(8,128)(2,1)}, bf16[192,1024]{1,0:T(8,128)(2,1)}, u32[]{:S(2)}, u32[]{:S(2)}) %collective-permute-start) | collective-permute-done | bytes 393248 | tf_op jit(solution)/shard_map/ppermute | solution.py:16
  84.8 1.9 %fusion.12 = bf16[1,192,1024]{2,1,0:T(8,128)(2,1)} fusion(bf16[192,1024]{1,0:T(8,128)(2,1)} %collective-permute-done, pred[]{:T(512)S(6)} %ge.3, bf16[192,2048]{1,0:T(8,128)(2,1)S(1)} %convolution_convert_fusion), kind=kLoop, calls=%fused_computation.24 | loop fusion | flops 983040 | bytes 1572865 | tf_op jit(solution)/shard_map/broadcast_in_dim | solution.py:137
  86.7 8.4 %all-to-all-done.3 = bf16[16,5,2048]{2,1,0:T(8,128)(2,1)S(1)} async-done(((bf16[16,5,2048]{2,1,0:T(8,128)(2,1)}), bf16[16,5,2048]{2,1,0:T(8,128)(2,1)S(1)}, u32[]{:S(2)}, u32[]{:S(2)}) %all-to-all-start.3) | async-done | bytes 327712 | tf_op jit(solution)/shard_map/all_to_all | solution.py:105
  95.3 1.8 %convolution_convert_fusion.1 = bf16[128,2048]{1,0:T(8,128)(2,1)} fusion(f32[20,128]{1,0:T(8,128)S(1)} %copy-done.8, f32[20,2048]{1,0:T(8,128)S(1)} %reshape.99), kind=kOutput, calls=%fused_computation.1 | convolution fusion | flops 63176704 | bytes 698368 | tf_op jit(solution)/shard_map/dot_general | solution.py:123
  (50 shorter events, 2.0 us)
Async XLA Ops:
  0.6 27.3 %copy-start = (bf16[1,2048,192]{1,2,0:T(8,128)(2,1)S(1)}, bf16[1,2048,192]{1,2,0:T(8,128)(2,1)}, u32[]{:S(2)}) copy-start(bf16[1,2048,192]{1,2,0:T(8,128)(2,1)} %param.12) | copy-start | bytes 2359300
  4.2 45.2 %copy-start.7 = (f32[20,128]{1,0:T(8,128)}, f32[20,128]{1,0:T(8,128)S(1)}, u32[]{:S(2)}) copy-start(f32[20,128]{1,0:T(8,128)S(1)} %convert_reduce_fusion.2) | copy-start | bytes 30724
  5.6 21.9 %copy-start.2 = (bf16[1,2048,192]{1,2,0:T(8,128)(2,1)S(1)}, bf16[1,2048,192]{1,2,0:T(8,128)(2,1)}, u32[]{:S(2)}) copy-start(bf16[1,2048,192]{1,2,0:T(8,128)(2,1)} %param.11) | copy-start | bytes 2359300
  27.9 1.7 %copy-start.1 = (bf16[1,192,2048]{2,1,0:T(8,128)(2,1)S(1)}, bf16[1,192,2048]{2,1,0:T(8,128)(2,1)}, u32[]{:S(2)}) copy-start(bf16[1,192,2048]{2,1,0:T(8,128)(2,1)} %param.13) | copy-start | bytes 2359300
  28.9 0.6 copy-start.5
  29.8 5.0 %copy-start.10 = (f32[128,8]{0,1:T(8,128)S(1)}, f32[128,8]{0,1:T(8,128)}, u32[]{:S(2)}) copy-start(f32[128,8]{0,1:T(8,128)} %param.10) | copy-start | bytes 12292
  30.8 18.6 %all-to-all-start.1 = ((bf16[16,5,2048]{2,1,0:T(8,128)(2,1)}), bf16[16,5,2048]{2,1,0:T(8,128)(2,1)S(1)}, u32[]{:S(2)}, u32[]{:S(2)}) async-start(bf16[16,5,2048]{2,1,0:T(8,128)(2,1)} %squeeze_stack_reshape.6), calls=%async_computation.1 | async-start | bytes 1048576 | tf_op jit(solution)/shard_map/all_to_all | solution.py:104
  35.2 16.2 %copy-start.11 = (f32[20]{0:T(128)}, f32[20]{0:T(128)S(1)}, u32[]{:S(2)}) copy-start(f32[20]{0:T(128)S(1)} %convolution_bitcast_fusion) | copy-start | bytes 244
  49.5 2.8 %copy-start.3 = (f32[20,2048]{1,0:T(8,128)}, f32[20,2048]{1,0:T(8,128)S(1)}, u32[]{:S(2)}) copy-start(f32[20,2048]{1,0:T(8,128)S(1)} %reshape.96) | copy-start | bytes 491524
  52.3 18.6 %all-to-all-start.2 = ((bf16[16,5,2048]{2,1,0:T(8,128)(2,1)}), bf16[16,5,2048]{2,1,0:T(8,128)(2,1)S(1)}, u32[]{:S(2)}, u32[]{:S(2)}) async-start(bf16[16,5,2048]{2,1,0:T(8,128)(2,1)} %bitcast.8), calls=%async_computation.2 | async-start | bytes 1048576 | tf_op jit(solution)/shard_map/all_to_all | solution.py:88
  72.6 2.3 %copy-start.6 = (f32[80,192]{1,0:T(8,128)S(1)}, f32[80,192]{1,0:T(8,128)}, u32[]{:S(2)}) copy-start(f32[80,192]{1,0:T(8,128)} %get-tuple-element.7) | copy-start | bytes 184324
  73.4 11.4 %collective-permute-start = (bf16[192,1024]{1,0:T(8,128)(2,1)}, bf16[192,1024]{1,0:T(8,128)(2,1)}, u32[]{:S(2)}, u32[]{:S(2)}) collective-permute-start(bf16[192,1024]{1,0:T(8,128)(2,1)} %broadcast_select_fusion), channel_id=1, source_target_pairs={{0,16},{16,0},{1,17},{17,1},{2,18},{18,2},{3,19},{19,3},{4,20},{20... | collective-permute-start | bytes 1179656 | tf_op jit(solution)/shard_map/ppermute | solution.py:16
  75.5 5.2 %copy-start.9 = (s32[128,8]{1,0:T(8,128)S(1)}, s32[128,8]{1,0:T(8,128)}, u32[]{:S(2)}) copy-start(s32[128,8]{1,0:T(8,128)} %copy.33) | copy-start | bytes 12292
  75.5 5.2 %copy-start.13 = (f32[20]{0:T(128)S(1)}, f32[20]{0:T(128)}, u32[]{:S(2)}) copy-start(f32[20]{0:T(128)} %get-tuple-element.4) | copy-start | bytes 244
  76.4 5.3 %copy-start.4 = (f32[20,2048]{1,0:T(8,128)S(1)}, f32[20,2048]{1,0:T(8,128)}, u32[]{:S(2)}) copy-start(f32[20,2048]{1,0:T(8,128)} %copy-done.3) | copy-start | bytes 491524
  76.4 5.3 %copy-start.8 = (f32[20,128]{1,0:T(8,128)S(1)}, f32[20,128]{1,0:T(8,128)}, u32[]{:S(2)}) copy-start(f32[20,128]{1,0:T(8,128)} %copy-done.7) | copy-start | bytes 30724
  76.4 5.3 %copy-start.12 = (f32[20]{0:T(128)S(1)}, f32[20]{0:T(128)}, u32[]{:S(2)}) copy-start(f32[20]{0:T(128)} %copy-done.11) | copy-start | bytes 244
  76.4 18.7 %all-to-all-start.3 = ((bf16[16,5,2048]{2,1,0:T(8,128)(2,1)}), bf16[16,5,2048]{2,1,0:T(8,128)(2,1)S(1)}, u32[]{:S(2)}, u32[]{:S(2)}) async-start(bf16[16,5,2048]{2,1,0:T(8,128)(2,1)} %squeeze_stack_reshape.7), calls=%async_computation.3 | async-start | bytes 1048576 | tf_op jit(solution)/shard_map/all_to_all | solution.py:105
where the time goes:
time: 97.8 us; the launch traced here: 97.1 us
  waiting for transfers between devices  37.5 us (38%)
  blocking collectives  21.8 us (22%)
  starting transfers between devices  13.9 us (14%)
  matrix products  10.7 us (11%)
  local copies, waits for them, and re-layouts  6.83 us (7%)
  other arithmetic  5.5 us (6%)
    all_to_all x1, blocking collectives, body(): lax.all_to_all(spread(slot_rows), 'expert', split_axis=0, concat_axis=0,...  21.8 us
    all_to_all x1, waiting for transfers between devices, body(): lax.all_to_all(stacked[0], 'expert', split_axis=0, concat_axis=0, tiled=T...  14.1 us
    all_to_all x1, waiting for transfers between devices, body(): lax.all_to_all(spread(slot_scaled), 'expert', split_axis=0, concat_axis=0...  13.7 us
    all_to_all x1, waiting for transfers between devices, body(): lax.all_to_all(stacked[1], 'expert', split_axis=0, concat_axis=0, tiled=T...  8.42 us
    all_to_all x1, starting transfers between devices, body(): lax.all_to_all(stacked[1], 'expert', split_axis=0, concat_axis=0, tiled=T...  4.22 us
    all_to_all x1, starting transfers between devices, body(): lax.all_to_all(stacked[0], 'expert', split_axis=0, concat_axis=0, tiled=T...  4.1 us
    all_to_all x1, starting transfers between devices, body(): lax.all_to_all(spread(slot_scaled), 'expert', split_axis=0, concat_axis=0...  4.1 us
  transfers between devices with their start and end apart: 4, of which 4 were waited for; matrix products, arithmetic and copies ran while one was open for 8% of the time, Pallas kernels for 0%

commit v1 on v0

v1 whole, which is shorter than its diff:
```python
import functools

import jax
import jax.numpy as jnp
from jax import lax
from jax.experimental import pallas as pl
from jax.experimental.pallas import tpu as pltpu
from jax.sharding import PartitionSpec as P

WS = 4
LANES = 128
BF16 = jnp.bfloat16
F32 = jnp.float32
MESH = pl.DeviceIdType.MESH


def dot(a, b, dims=((1,), (0,))):
    return lax.dot_general(a, b, (dims, ((), ())), preferred_element_type=F32)


def kernel(
    sections,
    devices,
    capacity,
    tokens_hbm,
    cot_hbm,
    ids_ref,
    gates_ref,
    gate_hbm,
    up_hbm,
    down_hbm,
    mixed_ref,
    token_ref,
    gate_grad_ref,
    down_grad_ref,
    tokens,
    cot,
    w_gate,
    w_up,
    w_down,
    wide_a,
    wide_b,
    slot_cot,
    sent,
    held,
    rows_in,
    rows_scaled,
    hidden_own,
    hidden_other,
    scaled_other,
    terms,
    from_core,
    to_x,
    from_x,
    to_owner,
    returned,
    load_sem,
    z_send,
    z_recv,
    f_send,
    f_recv,
    p_send,
    p_recv,
    a_send,
    a_recv,
    b_send,
    b_recv,
    c_send,
    c_recv,
):
    experts = devices // WS
    pieces = tokens.shape[1] // LANES
    tok_count, width = tokens.shape
    half = width // 2
    part = capacity * pieces
    slots = slot_cot.shape[0]
    row_count = devices * capacity
    section = lax.axis_index("pipe")
    me = lax.axis_index("expert")
    w, g = me // WS, me % WS
    x, core = g // 2, g % 2
    mirror = sections - 1 - section
    sibling = w * WS + x * 2 + (1 - core)
    across = w * WS + (1 - x) * 2 + core

    def owner(expert):
        return expert * WS + g

    def remote(src, dst, send, recv, pipe_pos, expert_pos):
        return pltpu.make_async_remote_copy(
            src_ref=src,
            dst_ref=dst,
            send_sem=send,
            recv_sem=recv,
            device_id=(pipe_pos, expert_pos),
            device_id_type=MESH,
        )

    loads = [
        pltpu.make_async_copy(src, dst, load_sem.at[i])
        for i, (src, dst) in enumerate(
            [
                (tokens_hbm, tokens),
                (cot_hbm, cot),
                (gate_hbm.at[0], w_gate),
                (up_hbm.at[0], w_up),
                (down_hbm.at[0], w_down),
            ]
        )
    ]
    for load in loads:
        load.start()
    barrier = pltpu.get_barrier_semaphore()
    for d in range(1, experts):
        pl.semaphore_signal(
            barrier,
            inc=1,
            device_id=(section, owner(lax.rem(w + d, experts))),
            device_id_type=MESH,
        )
    for target in ((section, sibling), (section, across), (mirror, me)):
        pl.semaphore_signal(barrier, inc=1, device_id=target, device_id_type=MESH)

    lane = lax.broadcasted_iota(jnp.int32, (tok_count, LANES), 1)
    lane_expert = jnp.where(lane < experts * capacity, lane // capacity, -1)
    lane_rank = (lane % capacity).astype(F32)
    ids = ids_ref[...]
    gates = gates_ref[...]
    chosen = ids.shape[1]
    named = [ids[:, k : k + 1] == lane_expert for k in range(chosen)]
    match = jnp.zeros((tok_count, LANES), F32)
    weight = jnp.zeros((tok_count, LANES), F32)
    for k in range(chosen):
        match += jnp.where(named[k], 1.0, 0.0)
        weight += jnp.where(named[k], gates[:, k : k + 1], 0.0)
    row_no = lax.broadcasted_iota(jnp.int32, (tok_count, tok_count), 0)
    col_no = lax.broadcasted_iota(jnp.int32, (tok_count, tok_count), 1)
    below = jnp.where(col_no < row_no, 1.0, 0.0).astype(BF16)
    earlier = dot(below, match.astype(BF16))
    pick = jnp.where((match > 0.5) & (earlier == lane_rank), 1.0, 0.0)
    pick_gate = pick * weight
    slot_gate = jnp.sum(pick_gate.T, axis=1, keepdims=True)[:slots]
    pick_rows = pick.T[:slots].astype(BF16)

    def to_wire(scratch, values, count):
        for j in range(pieces):
            scratch[pl.ds(j, count, stride=pieces), :] = values[
                :, j * LANES : (j + 1) * LANES
            ]

    loads[0].wait()
    to_wire(wide_a, dot(pick_rows, tokens[...]), slots)
    loads[1].wait()
    cot_rows = dot(pick_rows, cot[...])
    slot_cot[...] = cot_rows
    to_wire(wide_b, slot_gate * cot_rows, slots)
    for e in range(experts):
        sent[e, :part] = wide_a[e * part : (e + 1) * part].astype(BF16)
        sent[e, part:] = wide_b[e * part : (e + 1) * part].astype(BF16)
    held[w, g] = sent[w]
    pl.semaphore_wait(barrier, experts + 2)

    outgoing = []
    for d in range(experts - 1, 0, -1):
        to = lax.rem(w + d, experts)
        copy = remote(
            sent.at[to], held.at[w, g], z_send.at[d], z_recv.at[d], section, owner(to)
        )
        copy.start()
        outgoing.append(copy)
    g_core = x * 2 + (1 - core)
    g_across = (1 - x) * 2 + core
    g_far = (1 - x) * 2 + (1 - core)
    order = [0] + list(range(1, experts))
    for d in order:
        src = lax.rem(w - d + experts, experts)
        block = held.at[src, g]
        if d:
            remote(
                block, block, z_send.at[d], z_recv.at[d], section, me ^ 1
            ).wait_recv()
        for n, to in enumerate((across, sibling)):
            copy = remote(block, block, f_send.at[n, d], f_recv.at[n, d], section, to)
            copy.start()
            outgoing.append(copy)
    for d in order:
        src = lax.rem(w - d + experts, experts)
        block = held.at[src, g_across]
        remote(
            block, block, f_send.at[0, d], f_recv.at[0, d], section, across
        ).wait_recv()
        copy = remote(block, block, f_send.at[2, d], f_recv.at[2, d], section, sibling)
        copy.start()
        outgoing.append(copy)
    for d in order:
        src = lax.rem(w - d + experts, experts)
        for n, place in ((1, g_core), (2, g_far)):
            block = held.at[src, place]
            remote(
                block, block, f_send.at[n, d], f_recv.at[n, d], section, sibling
            ).wait_recv()

    for e in range(experts):
        for q in range(WS):
            at = (e * WS + q) * part
            wide_a[at : at + part] = held[e, q, :part].astype(F32)
            wide_b[at : at + part] = held[e, q, part:].astype(F32)
    for j in range(pieces):
        cols = slice(j * LANES, (j + 1) * LANES)
        pieces_at = pl.ds(j, row_count, stride=pieces)
        rows_scaled[:, cols] = wide_b[pieces_at, :].astype(BF16)
        rows_in[:, cols] = wide_a[pieces_at, :].astype(BF16)
    upper = jnp.where(section >= sections // 2, 1, 0)
    own_cols = pl.ds(pl.multiple_of(upper * half, half), half)
    other_cols = pl.ds(pl.multiple_of((1 - upper) * half, half), half)
    copy = remote(
        rows_scaled.at[:, other_cols],
        scaled_other,
        p_send.at[0],
        p_recv.at[0],
        mirror,
        me,
    )
    copy.start()
    outgoing.append(copy)
    mirrored = [copy]

    loads[2].wait()
    loads[3].wait()
    loads[4].wait()
    gate_pre = dot(rows_in[...], w_gate[...])
    up_pre = dot(rows_in[...], w_up[...])
    sigmoid = jax.nn.sigmoid(gate_pre)
    activated = gate_pre * sigmoid
    slope = sigmoid * (1.0 + gate_pre * (1.0 - sigmoid))
    hidden = (activated * up_pre).astype(BF16)
    hidden_own[...] = hidden
    copy = remote(
        hidden_own, hidden_other, p_send.at[1], p_recv.at[1], mirror, me
    )
    copy.start()
    outgoing.append(copy)
    mirrored.append(copy)
    to_wire(wide_a, dot(hidden, w_down[...]), row_count)
    hidden_grad = dot(rows_scaled[...], w_down[...], ((1,), (1,)))
    grad_gate = (hidden_grad * up_pre * slope).astype(BF16)
    grad_up = (hidden_grad * activated).astype(BF16)
    transposed = ((1,), (1,))
    to_wire(
        wide_b,
        dot(grad_gate, w_gate[...], transposed) + dot(grad_up, w_up[...], transposed),
        row_count,
    )
    for q in range(WS):
        for e in range(experts):
            at = (e * WS + q) * part
            terms[q % 2, q // 2, e, :part] = wide_a[at : at + part].astype(BF16)
            terms[q % 2, q // 2, e, part:] = wide_b[at : at + part].astype(BF16)

    cores = []
    for n, side in enumerate((1 - x, x)):
        copy = remote(
            terms.at[1 - core, side],
            from_core.at[side],
            a_send.at[n],
            a_recv.at[n],
            section,
            sibling,
        )
        copy.start()
        outgoing.append(copy)
        cores.append(copy)
    cores[0].wait_recv()
    crossing = []
    for d in order:
        e = lax.rem(w + d, experts)
        to_x[e] = (
            terms[core, 1 - x, e].astype(F32) + from_core[1 - x, e].astype(F32)
        ).astype(BF16)
        copy = remote(
            to_x.at[e], from_x.at[e], b_send.at[d], b_recv.at[d], section, across
        )
        copy.start()
        outgoing.append(copy)
        crossing.append(copy)
    cores[1].wait_recv()
    returns = []
    for n, d in enumerate(order):
        e = lax.rem(w + d, experts)
        crossing[n].wait_recv()
        total = (
            terms[core, x, e].astype(F32)
            + from_core[x, e].astype(F32)
            + from_x[e].astype(F32)
        ).astype(BF16)
        if d == 0:
            returned[w] = total
        else:
            to_owner[e] = total
            copy = remote(
                to_owner.at[e],
                returned.at[w],
                c_send.at[d],
                c_recv.at[d],
                section,
                owner(e),
            )
            copy.start()
            outgoing.append(copy)
            returns.append(copy)

    down_own = dot(hidden_own[...], rows_scaled[:, own_cols], ((0,), (0,)))
    for copy in mirrored:
        copy.wait_recv()
    down_other = dot(hidden_other[...], scaled_other[...], ((0,), (0,)))
    down_grad_ref[0] = (
        down_own.astype(BF16).astype(F32) + down_other.astype(BF16).astype(F32)
    ).astype(BF16)

    for copy in returns:
        copy.wait_recv()
    for e in range(experts):
        wide_a[e * part : (e + 1) * part] = returned[e, :part].astype(F32)
        wide_b[e * part : (e + 1) * part] = returned[e, part:].astype(F32)
    if slots > experts * capacity:
        rest = slice(experts * part, slots * pieces)
        zero = jnp.zeros((slots * pieces - experts * part, LANES), F32)
        wide_a[rest] = zero
        wide_b[rest] = zero
    pick_narrow = pick[:, :slots].astype(BF16)
    gate_high = pick_gate[:, :slots].astype(BF16)
    left = pick_gate[:, :slots] - gate_high.astype(F32)
    gate_mid = left.astype(BF16)
    gate_low = (left - gate_mid.astype(F32)).astype(BF16)
    value = jnp.zeros((slots, LANES), F32)
    for j in range(pieces):
        cols = slice(j * LANES, (j + 1) * LANES)
        out = wide_a[pl.ds(j, slots, stride=pieces), :]
        narrow = out.astype(BF16)
        mixed_ref[:, cols] = (
            dot(gate_low, narrow) + dot(gate_mid, narrow) + dot(gate_high, narrow)
        ).astype(BF16)
        value += slot_cot[:, cols] * out
        grad = wide_b[pl.ds(j, slots, stride=pieces), :].astype(BF16)
        token_ref[:, cols] = dot(pick_narrow, grad).astype(BF16)
    column = jnp.sum(value, axis=1, keepdims=True)
    column = jnp.concatenate([column, jnp.zeros((LANES - slots, 1), F32)], axis=0)
    spread = pick * jnp.broadcast_to(column, (LANES, tok_count)).T
    for k in range(chosen):
        gate_grad_ref[:, k : k + 1] = jnp.sum(
            jnp.where(named[k], spread, 0.0), axis=1, keepdims=True
        )
    for copy in outgoing:
        copy.wait_send()


def body(sections, devices, tokens, cotangent, expert_ids, gates, w_gate, w_up, w_down):
    tok_count, width = tokens.shape
    capacity = tok_count // 24
    experts = devices // WS
    units = w_gate.shape[2]
    pieces = width // LANES
    part = capacity * pieces
    slots = -(-experts * capacity // 16) * 16
    rows = devices * capacity
    dma = pltpu.SemaphoreType.DMA
    anywhere = pl.BlockSpec(memory_space=pl.ANY)
    vmem = pl.BlockSpec(memory_space=pltpu.VMEM)
    return pl.pallas_call(
        functools.partial(kernel, sections, devices, capacity),
        out_shape=(
            jax.ShapeDtypeStruct((tok_count, width), BF16),
            jax.ShapeDtypeStruct((tok_count, width), BF16),
            jax.ShapeDtypeStruct(gates.shape, F32),
            jax.ShapeDtypeStruct((1, units, width // 2), BF16),
        ),
        in_specs=[anywhere, anywhere, vmem, vmem, anywhere, anywhere, anywhere],
        out_specs=(vmem, vmem, vmem, vmem),
        scratch_shapes=[
            pltpu.VMEM((tok_count, width), BF16),
            pltpu.VMEM((tok_count, width), BF16),
            pltpu.VMEM((width, units), BF16),
            pltpu.VMEM((width, units), BF16),
            pltpu.VMEM((units, width), BF16),
            pltpu.VMEM((rows * pieces, LANES), F32),
            pltpu.VMEM((rows * pieces, LANES), F32),
            pltpu.VMEM((slots, width), F32),
            pltpu.VMEM((experts, 2 * part, LANES), BF16),
            pltpu.VMEM((experts, WS, 2 * part, LANES), BF16),
            pltpu.VMEM((rows, width), BF16),
            pltpu.VMEM((rows, width), BF16),
            pltpu.VMEM((rows, units), BF16),
            pltpu.VMEM((rows, units), BF16),
            pltpu.VMEM((rows, width // 2), BF16),
            pltpu.VMEM((2, 2, experts, 2 * part, LANES), BF16),
            pltpu.VMEM((2, experts, 2 * part, LANES), BF16),
            pltpu.VMEM((experts, 2 * part, LANES), BF16),
            pltpu.VMEM((experts, 2 * part, LANES), BF16),
            pltpu.VMEM((experts, 2 * part, LANES), BF16),
            pltpu.VMEM((experts, 2 * part, LANES), BF16),
            dma((5,)),
            dma((experts,)),
            dma((experts,)),
            dma((3, experts)),
            dma((3, experts)),
            dma((2,)),
            dma((2,)),
            dma((2,)),
            dma((2,)),
            dma((experts,)),
            dma((experts,)),
            dma((experts,)),
            dma((experts,)),
        ],
        compiler_params=pltpu.CompilerParams(
            collective_id=0, has_side_effects=True, vmem_limit_bytes=48 << 20
        ),
        cost_estimate=pl.CostEstimate(
            flops=16 * rows * width * units,
            bytes_accessed=6 * width * units + 12 * tok_count * width,
            transcendentals=rows * units,
        ),
    )(tokens, cotangent, expert_ids, gates, w_gate, w_up, w_down)


def solution(mesh):
    rows = P(("pipe", "expert"), None)
    return jax.shard_map(
        functools.partial(body, mesh.shape["pipe"], mesh.shape["expert"]),
        mesh=mesh,
        in_specs=(
            rows,
            rows,
            rows,
            rows,
            P("pipe", None, "expert"),
            P("pipe", None, "expert"),
            P("pipe", "expert", None),
        ),
        out_specs=(rows, rows, rows, P("pipe", "expert", None)),
        check_vma=False,
    )
```

time: 97.8 us -> 42.3 us (0.43)
  waiting for transfers between devices: 37.5 us -> 0 us
  Pallas kernels: 0 us -> 27.8 us
  blocking collectives: 21.8 us -> 0 us
  starting transfers between devices: 13.9 us -> 0 us
  matrix products: 10.7 us -> 0 us
  local copies, waits for them, and re-layouts: 6.83 us -> 13.4 us
  other arithmetic: 5.5 us -> 0 us
    all_to_all x3 -> x0, waiting for transfers between devices: 36.3 us -> none  [the longest x1 14.1 us: body(): lax.all_to_all(stacked[0], 'expert', split_axis=0, concat_axis=0, tiled=T...]
    pallas_call x0 -> x1, Pallas kernels: none -> 27.8 us  [body(): pl.pallas_call(functools.partial(kernel, sections, devices, capacity), ou...]
    all_to_all x1 -> x0, blocking collectives: 21.8 us -> none  [body(): lax.all_to_all(spread(slot_rows), 'expert', split_axis=0, concat_axis=0,...]
    all_to_all x3 -> x0, starting transfers between devices: 12.4 us -> none  [the longest x1 4.22 us: body(): lax.all_to_all(stacked[1], 'expert', split_axis=0, concat_axis=0, tiled=T...]
    dot_general x12 -> x0, matrix products: 10.7 us -> none  [the longest x1 1.93 us: body(): jnp.dot(pick_narrow, cotangent, preferred_element_type=jnp.float32)]
    unnamed x30 -> x23, local copies, waits for them, and re-layouts: 1.65 us -> 11.9 us
    broadcast_in_dim x1 -> x0, other arithmetic: 1.94 us -> none  [body(): (kept_half.astype(jnp.float32) + partner_part).astype(jnp.bfloat16)[None]]
    another operation x2 -> x0, local copies, waits for them, and re-layouts: 1.85 us -> none  [the longest x1 0.93 us: body(): stacked[0]]
  transfers between devices with their start and end apart: 4 -> 0, of which waited for: 4 -> 0; matrix products, arithmetic and copies ran while one was open for 8% -> 0% of each run, Pallas kernels for 0% -> 0%
where the time goes in v1:
time: 42.3 us; the launch traced here: 41.9 us
  Pallas kernels  27.8 us (66%)
  local copies, waits for them, and re-layouts  13.4 us (32%)
  between operations  0.7 us (2%)
    pallas_call x1, Pallas kernels, body(): pl.pallas_call(functools.partial(kernel, sections, devices, capacity), ou...  27.8 us
    unnamed x23, local copies, waits for them, and re-layouts  11.9 us
    pallas_call x1, local copies, waits for them, and re-layouts, body(): pl.pallas_call(functools.partial(kernel, sections, devices, capacity), ou...  1.5 us

profile of v1, /device:TPU:0, one launch (start us, length us, event | category | flops | bytes accessed | tf_op | source)
XLA Modules:
  0.0 41.9 jit_solution(11234619183487232037)
XLA Ops:
  0.6 0.0 copy-start.7
  0.6 0.8 %copy.11.ids_ref = s32[128,8]{1,0:T(8,128)S(1)} copy(s32[128,8]{0,1:T(8,128)} %param.9) | data formatting | bytes 8192 | tf_op args[2]
  1.4 0.0 copy-done.7
  1.4 0.1 copy.12.gates_ref
  1.5 1.4 %copy.13.gate_hbm = bf16[1,2048,192]{2,1,0:T(8,128)(2,1)S(1)} copy(bf16[1,2048,192]{1,2,0:T(8,128)(2,1)} %param.11) | data formatting | bytes 1572864 | tf_op args[4]
  3.0 0.0 copy-start
  3.0 1.5 %copy.14.up_hbm = bf16[1,2048,192]{2,1,0:T(8,128)(2,1)S(1)} copy(bf16[1,2048,192]{1,2,0:T(8,128)(2,1)} %param.12) | data formatting | bytes 1572864 | tf_op args[5]
  4.5 0.0 copy-done
  4.5 0.0 copy-start.2
  4.5 1.0 %copy-done.2 = bf16[128,2048]{1,0:T(8,128)(2,1)S(1)} copy-done((bf16[128,2048]{1,0:T(8,128)(2,1)S(1)}, bf16[128,2048]{1,0:T(8,128)(2,1)}, u32[]{:S(2)}) %copy-start.2) | copy-done | bytes 524312
  5.6 0.0 copy-start.3
  5.6 1.0 %copy-done.3 = bf16[128,2048]{1,0:T(8,128)(2,1)S(1)} copy-done((bf16[128,2048]{1,0:T(8,128)(2,1)S(1)}, bf16[128,2048]{1,0:T(8,128)(2,1)}, u32[]{:S(2)}) %copy-start.3) | copy-done | bytes 524312
  6.6 27.8 %shard_map.102 = (bf16[128,2048]{1,0:T(8,128)(2,1)S(1)}, bf16[128,2048]{1,0:T(8,128)(2,1)S(1)}, f32[128,8]{1,0:T(8,128)S(1)}, bf16[1,192,1024]{2,1,0:T(8,128)(2,1)S(1)}) custom-call(bf16[128,2048]{1,0:T(8,128)(2,1)S(1)} %copy-done.2, bf16[128,2048]{1,0:T(8,128)(2,1)S(1)} %copy-done.3, s32[128,8]{1,0:T(8,128)S(1)} %copy.11.ids_ref, ...), custom_call_target="tpu_custom_call" | custom-call | flops 503316480 | bytes 5505024 | tf_op jit(solution)/shard_map/pallas_call | solution.py:369
  34.4 0.0 copy-start.1
  34.4 0.8 %copy-done.1 = bf16[128,2048]{1,0:T(8,128)(2,1)} copy-done((bf16[128,2048]{1,0:T(8,128)(2,1)}, bf16[128,2048]{1,0:T(8,128)(2,1)S(1)}, u32[]{:S(2)}) %copy-start.1) | copy-done | bytes 524312
  35.2 0.0 copy-start.4
  35.2 0.7 %copy-done.4 = bf16[1,192,1024]{2,1,0:T(8,128)(2,1)} copy-done((bf16[1,192,1024]{2,1,0:T(8,128)(2,1)}, bf16[1,192,1024]{2,1,0:T(8,128)(2,1)S(1)}, u32[]{:S(2)}) %copy-start.4) | copy-done | bytes 393240
  36.0 0.0 copy-start.6
  36.0 0.6 %copy-done.6 = f32[128,8]{1,0:T(8,128)} copy-done((f32[128,8]{1,0:T(8,128)}, f32[128,8]{1,0:T(8,128)S(1)}, u32[]{:S(2)}) %copy-start.6) | copy-done | bytes 4120
  36.6 1.5 %copy.15 = f32[128,8]{0,1:T(8,128)} copy(f32[128,8]{1,0:T(8,128)} %copy-done.6) | data formatting | bytes 8192 | tf_op jit(solution)/shard_map/pallas_call | solution.py:369
  38.1 1.9 %copy.19 = bf16[128,2048]{1,0:T(8,128)(2,1)} copy(bf16[128,2048]{1,0:T(8,128)(2,1)} %copy-done.1) | data formatting | bytes 1048576
  40.0 0.0 copy-start.5
  40.0 0.8 %copy.20 = bf16[128,2048]{1,0:T(8,128)(2,1)} copy(bf16[128,2048]{1,0:T(8,128)(2,1)S(1)} %get-tuple-element.13) | data formatting | bytes 1048576
  40.8 0.4 copy-done.5
  41.2 0.7 %copy.21 = bf16[1,192,1024]{2,1,0:T(8,128)(2,1)} copy(bf16[1,192,1024]{2,1,0:T(8,128)(2,1)S(1)} %copy-done.5) | data formatting | bytes 786432
Async XLA Ops:
  0.6 0.8 %copy-start.7 = (f32[128,8]{0,1:T(8,128)S(1)}, f32[128,8]{0,1:T(8,128)}, u32[]{:S(2)}) copy-start(f32[128,8]{0,1:T(8,128)} %param.10) | copy-start | bytes 12292
  3.0 1.5 %copy-start = (bf16[1,192,2048]{2,1,0:T(8,128)(2,1)S(1)}, bf16[1,192,2048]{2,1,0:T(8,128)(2,1)}, u32[]{:S(2)}) copy-start(bf16[1,192,2048]{2,1,0:T(8,128)(2,1)} %down_hbm.1) | copy-start | bytes 2359300
  4.5 1.0 %copy-start.2 = (bf16[128,2048]{1,0:T(8,128)(2,1)S(1)}, bf16[128,2048]{1,0:T(8,128)(2,1)}, u32[]{:S(2)}) copy-start(bf16[128,2048]{1,0:T(8,128)(2,1)} %tokens_hbm.1) | copy-start | bytes 1572868
  5.6 1.0 %copy-start.3 = (bf16[128,2048]{1,0:T(8,128)(2,1)S(1)}, bf16[128,2048]{1,0:T(8,128)(2,1)}, u32[]{:S(2)}) copy-start(bf16[128,2048]{1,0:T(8,128)(2,1)} %cot_hbm.1) | copy-start | bytes 1572868
  34.4 0.8 %copy-start.1 = (bf16[128,2048]{1,0:T(8,128)(2,1)}, bf16[128,2048]{1,0:T(8,128)(2,1)S(1)}, u32[]{:S(2)}) copy-start(bf16[128,2048]{1,0:T(8,128)(2,1)S(1)} %get-tuple-element.12) | copy-start | bytes 1572868
  35.2 0.7 %copy-start.4 = (bf16[1,192,1024]{2,1,0:T(8,128)(2,1)}, bf16[1,192,1024]{2,1,0:T(8,128)(2,1)S(1)}, u32[]{:S(2)}) copy-start(bf16[1,192,1024]{2,1,0:T(8,128)(2,1)S(1)} %get-tuple-element.15) | copy-start | bytes 1179652
  36.0 0.6 %copy-start.6 = (f32[128,8]{1,0:T(8,128)}, f32[128,8]{1,0:T(8,128)S(1)}, u32[]{:S(2)}) copy-start(f32[128,8]{1,0:T(8,128)S(1)} %get-tuple-element.6) | copy-start | bytes 12292
  40.0 1.2 %copy-start.5 = (bf16[1,192,1024]{2,1,0:T(8,128)(2,1)S(1)}, bf16[1,192,1024]{2,1,0:T(8,128)(2,1)}, u32[]{:S(2)}) copy-start(bf16[1,192,1024]{2,1,0:T(8,128)(2,1)} %copy-done.4) | copy-start | bytes 1179652

commit v2 on v1

v2 whole, which is shorter than its diff:
```python
import functools

import jax
import jax.numpy as jnp
from jax import lax
from jax.experimental import pallas as pl
from jax.experimental.pallas import tpu as pltpu
from jax.sharding import PartitionSpec as P

WS = 4
LANES = 128
BF16 = jnp.bfloat16
F32 = jnp.float32
MESH = pl.DeviceIdType.MESH


def dot(a, b, dims=((1,), (0,))):
    return lax.dot_general(a, b, (dims, ((), ())), preferred_element_type=F32)


def named_slots(ids, slots, experts, capacity):
    slot = lax.broadcasted_iota(jnp.int32, (slots, ids.shape[1]), 0)
    slot_expert = jnp.where(slot < experts * capacity, slot // capacity, -1)
    return [ids[k : k + 1, :] == slot_expert for k in range(ids.shape[0])]


def moe_kernel(
    sections,
    devices,
    capacity,
    tokens_hbm,
    cot_hbm,
    ids_ref,
    gates_ref,
    gate_hbm,
    up_hbm,
    down_hbm,
    returned_ref,
    pick_ref,
    pick_gate_ref,
    slot_cot_ref,
    down_grad_ref,
    tokens,
    cot,
    w_gate,
    w_up,
    w_down,
    wide_a,
    wide_b,
    sent,
    held,
    rows_in,
    rows_scaled,
    hidden_own,
    hidden_other,
    scaled_other,
    terms,
    from_core,
    to_x,
    from_x,
    to_owner,
    returned,
    load_sem,
    z_send,
    z_recv,
    f_send,
    f_recv,
    p_send,
    p_recv,
    a_send,
    a_recv,
    b_send,
    b_recv,
    c_send,
    c_recv,
):
    experts = devices // WS
    tok_count, width = tokens.shape
    pieces = width // LANES
    half = width // 2
    part = capacity * pieces
    slots = slot_cot_ref.shape[0]
    row_count = devices * capacity
    section = lax.axis_index("pipe")
    me = lax.axis_index("expert")
    w, g = me // WS, me % WS
    x, core = g // 2, g % 2
    mirror = sections - 1 - section
    sibling = w * WS + x * 2 + (1 - core)
    across = w * WS + (1 - x) * 2 + core
    transposed = ((1,), (1,))

    def owner(expert):
        return expert * WS + g

    def remote(src, dst, send, recv, pipe_pos, expert_pos):
        return pltpu.make_async_remote_copy(
            src_ref=src,
            dst_ref=dst,
            send_sem=send,
            recv_sem=recv,
            device_id=(pipe_pos, expert_pos),
            device_id_type=MESH,
        )

    outgoing = []

    def push(*args):
        copy = remote(*args)
        copy.start()
        outgoing.append(copy)
        return copy

    loads = [
        pltpu.make_async_copy(src, dst, load_sem.at[i])
        for i, (src, dst) in enumerate(
            [
                (tokens_hbm, tokens),
                (cot_hbm, cot),
                (gate_hbm.at[0], w_gate),
                (up_hbm.at[0], w_up),
                (down_hbm.at[0], w_down),
            ]
        )
    ]
    for load in loads:
        load.start()
    barrier = pltpu.get_barrier_semaphore()
    for d in range(1, experts):
        pl.semaphore_signal(
            barrier,
            inc=1,
            device_id=(section, owner(lax.rem(w + d, experts))),
            device_id_type=MESH,
        )
    for target in ((section, sibling), (section, across), (mirror, me)):
        pl.semaphore_signal(barrier, inc=1, device_id=target, device_id_type=MESH)

    ids = ids_ref[...]
    gates = gates_ref[...]
    named = named_slots(ids, slots, experts, capacity)
    match = jnp.zeros((slots, tok_count), F32)
    weight = jnp.zeros((slots, tok_count), F32)
    for k, here in enumerate(named):
        match += jnp.where(here, 1.0, 0.0)
        weight += jnp.where(here, gates[k : k + 1, :], 0.0)
    row_no = lax.broadcasted_iota(jnp.int32, (tok_count, tok_count), 0)
    col_no = lax.broadcasted_iota(jnp.int32, (tok_count, tok_count), 1)
    before = jnp.where(row_no < col_no, 1.0, 0.0).astype(BF16)
    earlier = dot(match.astype(BF16), before)
    slot = lax.broadcasted_iota(jnp.int32, (slots, tok_count), 0)
    slot_rank = (slot % capacity).astype(F32)
    pick = jnp.where((match > 0.5) & (earlier == slot_rank), 1.0, 0.0)
    pick_gate = pick * weight
    slot_gate = jnp.sum(pick_gate, axis=1, keepdims=True)
    pick_rows = pick.astype(BF16)

    def to_wire(scratch, values, count):
        for j in range(pieces):
            scratch[pl.ds(j, count, stride=pieces), :] = values[
                :, j * LANES : (j + 1) * LANES
            ]

    order = range(experts)
    far_first = range(experts - 1, 0, -1)
    spots = {
        "own": g,
        "core": x * 2 + (1 - core),
        "across": (1 - x) * 2 + core,
        "far": (1 - x) * 2 + (1 - core),
    }

    def dispatch(kind, scratch):
        for e in range(experts):
            sent[kind, e] = scratch[e * part : (e + 1) * part].astype(BF16)
        held[kind, 0, g] = sent[kind, w]

    def send_z(kind):
        for d in far_first:
            to = lax.rem(w + d, experts)
            push(
                sent.at[kind, to],
                held.at[kind, d, g],
                z_send.at[kind, d],
                z_recv.at[kind, d],
                section,
                owner(to),
            )

    def arrive(kind, hop, d, spot):
        block = held.at[kind, d, spots[spot]]
        if hop == 3:
            pair = (z_send.at[kind, d], z_recv.at[kind, d])
        else:
            pair = (f_send.at[kind, hop, d], f_recv.at[kind, hop, d])
        remote(block, block, *pair, section, sibling).wait_recv()

    def forward(kind, hop, d, spot, to):
        block = held.at[kind, d, spots[spot]]
        push(block, block, f_send.at[kind, hop, d], f_recv.at[kind, hop, d], section, to)

    def spread(kind):
        for d in order:
            if d:
                arrive(kind, 3, d, "own")
            forward(kind, 0, d, "own", across)
            forward(kind, 1, d, "own", sibling)

    def pass_on(kind):
        for d in order:
            arrive(kind, 0, d, "across")
            forward(kind, 2, d, "across", sibling)

    def collect(kind, scratch, rows):
        for d in order:
            arrive(kind, 1, d, "core")
            arrive(kind, 2, d, "far")
        for d in order:
            for q in range(WS):
                at = (d * WS + q) * part
                scratch[at : at + part] = held[kind, d, q].astype(F32)
        for j in range(pieces):
            rows[:, j * LANES : (j + 1) * LANES] = scratch[
                pl.ds(j, row_count, stride=pieces), :
            ].astype(BF16)

    def fold_cores(kind, scratch):
        for q in range(WS):
            for d in order:
                at = (d * WS + q) * part
                terms[kind, q % 2, q // 2, d] = scratch[at : at + part].astype(BF16)
        return [
            push(
                terms.at[kind, 1 - core, side],
                from_core.at[kind, side],
                a_send.at[kind, n],
                a_recv.at[kind, n],
                section,
                sibling,
            )
            for n, side in enumerate((1 - x, x))
        ]

    def fold_x(kind, cores):
        cores[0].wait_recv()
        crossing = []
        for d in far_first:
            to_x[kind, d] = (
                terms[kind, core, 1 - x, d].astype(F32)
                + from_core[kind, 1 - x, d].astype(F32)
            ).astype(BF16)
            crossing.append((d, push_x(kind, d)))
        to_x[kind, 0] = (
            terms[kind, core, 1 - x, 0].astype(F32)
            + from_core[kind, 1 - x, 0].astype(F32)
        ).astype(BF16)
        crossing.append((0, push_x(kind, 0)))
        cores[1].wait_recv()
        return crossing

    def push_x(kind, d):
        return push(
            to_x.at[kind, d],
            from_x.at[kind, d],
            b_send.at[kind, d],
            b_recv.at[kind, d],
            section,
            across,
        )

    def give_back(kind, crossing):
        returns = []
        for d, copy in crossing:
            copy.wait_recv()
            total = (
                terms[kind, core, x, d].astype(F32)
                + from_core[kind, x, d].astype(F32)
                + from_x[kind, d].astype(F32)
            ).astype(BF16)
            if d == 0:
                returned[kind, w] = total
            else:
                to_owner[kind, d] = total
                returns.append(
                    push(
                        to_owner.at[kind, d],
                        returned.at[kind, w],
                        c_send.at[kind, d],
                        c_recv.at[kind, d],
                        section,
                        owner(lax.rem(w + experts - d, experts)),
                    )
                )
        return returns

    loads[0].wait()
    to_wire(wide_a, dot(pick_rows, tokens[...]), slots)
    dispatch(0, wide_a)
    pl.semaphore_wait(barrier, experts + 2)
    send_z(0)
    loads[1].wait()
    cot_rows = dot(pick_rows, cot[...])
    to_wire(wide_b, slot_gate * cot_rows, slots)
    dispatch(1, wide_b)
    send_z(1)
    spread(0)
    slot_cot_ref[...] = cot_rows
    pick_ref[...] = pick
    pick_gate_ref[...] = pick_gate
    spread(1)
    pass_on(0)
    loads[2].wait()
    loads[3].wait()
    loads[4].wait()
    collect(0, wide_a, rows_in)
    gate_pre = dot(rows_in[...], w_gate[...], transposed)
    up_pre = dot(rows_in[...], w_up[...], transposed)
    sigmoid = jax.nn.sigmoid(gate_pre)
    activated = gate_pre * sigmoid
    slope = sigmoid * (1.0 + gate_pre * (1.0 - sigmoid))
    hidden = (activated * up_pre).astype(BF16)
    hidden_own[...] = hidden
    pass_on(1)
    to_wire(wide_a, dot(hidden, w_down[...]), row_count)
    out_cores = fold_cores(0, wide_a)
    mirrored = [push(hidden_own, hidden_other, p_send.at[1], p_recv.at[1], mirror, me)]

    collect(1, wide_b, rows_scaled)
    upper = jnp.where(section >= sections // 2, 1, 0)
    own_cols = pl.ds(pl.multiple_of(upper * half, half), half)
    other_cols = pl.ds(pl.multiple_of((1 - upper) * half, half), half)
    mirrored.append(
        push(
            rows_scaled.at[:, other_cols],
            scaled_other,
            p_send.at[0],
            p_recv.at[0],
            mirror,
            me,
        )
    )
    out_crossing = fold_x(0, out_cores)
    hidden_grad = dot(rows_scaled[...], w_down[...], transposed)
    grad_gate = (hidden_grad * up_pre * slope).astype(BF16)
    grad_up = (hidden_grad * activated).astype(BF16)
    to_wire(
        wide_b,
        dot(grad_gate, w_gate[...]) + dot(grad_up, w_up[...]),
        row_count,
    )
    grad_cores = fold_cores(1, wide_b)
    returns = give_back(0, out_crossing)
    grad_crossing = fold_x(1, grad_cores)
    down_own = dot(hidden_own[...], rows_scaled[:, own_cols], ((0,), (0,)))
    down_own = down_own.astype(BF16)
    returns += give_back(1, grad_crossing)
    for copy in mirrored:
        copy.wait_recv()
    down_other = dot(hidden_other[...], scaled_other[...], ((0,), (0,)))
    down_grad_ref[0] = (
        down_own.astype(F32) + down_other.astype(BF16).astype(F32)
    ).astype(BF16)
    for copy in returns:
        copy.wait_recv()
    returned_ref[...] = returned[...]
    for copy in outgoing:
        copy.wait_send()


def combine_kernel(
    experts,
    capacity,
    returned_ref,
    pick_ref,
    pick_gate_ref,
    slot_cot_ref,
    ids_ref,
    down_ref,
    mixed_ref,
    token_ref,
    gate_grad_ref,
    down_grad_ref,
    wide_a,
    wide_b,
):
    slots, width = slot_cot_ref.shape
    pieces = width // LANES
    part = capacity * pieces
    down_grad_ref[...] = down_ref[...]
    for e in range(experts):
        wide_a[e * part : (e + 1) * part] = returned_ref[0, e].astype(F32)
        wide_b[e * part : (e + 1) * part] = returned_ref[1, e].astype(F32)
    if slots > experts * capacity:
        rest = slice(experts * part, slots * pieces)
        zero = jnp.zeros((slots * pieces - experts * part, LANES), F32)
        wide_a[rest] = zero
        wide_b[rest] = zero
    pick = pick_ref[...]
    pick_gate = pick_gate_ref[...]
    turned = pick_gate.T
    high = turned.astype(BF16)
    left = turned - high.astype(F32)
    mid = left.astype(BF16)
    low = (left - mid.astype(F32)).astype(BF16)
    narrow_pick = pick.T.astype(BF16)
    value = jnp.zeros((slots, LANES), F32)
    outs = []
    grads = []
    for j in range(pieces):
        cols = slice(j * LANES, (j + 1) * LANES)
        out = wide_a[pl.ds(j, slots, stride=pieces), :]
        value += slot_cot_ref[:, cols] * out
        outs.append(out.astype(BF16))
        grads.append(wide_b[pl.ds(j, slots, stride=pieces), :].astype(BF16))
    for j in range(0, pieces, 4):
        cols = slice(j * LANES, (j + 4) * LANES)
        out = jnp.concatenate(outs[j : j + 4], axis=1)
        grad = jnp.concatenate(grads[j : j + 4], axis=1)
        mixed_ref[:, cols] = (dot(low, out) + dot(mid, out) + dot(high, out)).astype(
            BF16
        )
        token_ref[:, cols] = dot(narrow_pick, grad).astype(BF16)
    spread = pick * jnp.sum(value, axis=1, keepdims=True)
    for k, here in enumerate(named_slots(ids_ref[...], slots, experts, capacity)):
        gate_grad_ref[k : k + 1, :] = jnp.sum(
            jnp.where(here, spread, 0.0), axis=0, keepdims=True
        )


def body(sections, devices, tokens, cotangent, expert_ids, gates, w_gate, w_up, w_down):
    tok_count, width = tokens.shape
    capacity = tok_count // 24
    experts = devices // WS
    units = w_gate.shape[2]
    pieces = width // LANES
    part = capacity * pieces
    slots = -(-experts * capacity // 16) * 16
    rows = devices * capacity
    dma = pltpu.SemaphoreType.DMA
    far = pl.BlockSpec(memory_space=pltpu.HBM)
    vmem = pl.BlockSpec(memory_space=pltpu.VMEM)
    ids_turned = expert_ids.T
    returned, pick, pick_gate, slot_cot, down = pl.pallas_call(
        functools.partial(moe_kernel, sections, devices, capacity),
        out_shape=(
            jax.ShapeDtypeStruct((2, experts, part, LANES), BF16),
            jax.ShapeDtypeStruct((slots, tok_count), F32),
            jax.ShapeDtypeStruct((slots, tok_count), F32),
            jax.ShapeDtypeStruct((slots, width), F32),
            jax.ShapeDtypeStruct((1, units, width // 2), BF16),
        ),
        in_specs=[far, far, vmem, vmem, far, far, far],
        out_specs=(vmem,) * 5,
        scratch_shapes=[
            pltpu.VMEM((tok_count, width), BF16),
            pltpu.VMEM((tok_count, width), BF16),
            pltpu.VMEM((units, width), BF16),
            pltpu.VMEM((units, width), BF16),
            pltpu.VMEM((units, width), BF16),
            pltpu.VMEM((rows * pieces, LANES), F32),
            pltpu.VMEM((rows * pieces, LANES), F32),
            pltpu.VMEM((2, experts, part, LANES), BF16),
            pltpu.VMEM((2, experts, WS, part, LANES), BF16),
            pltpu.VMEM((rows, width), BF16),
            pltpu.VMEM((rows, width), BF16),
            pltpu.VMEM((rows, units), BF16),
            pltpu.VMEM((rows, units), BF16),
            pltpu.VMEM((rows, width // 2), BF16),
            pltpu.VMEM((2, 2, 2, experts, part, LANES), BF16),
            pltpu.VMEM((2, 2, experts, part, LANES), BF16),
            pltpu.VMEM((2, experts, part, LANES), BF16),
            pltpu.VMEM((2, experts, part, LANES), BF16),
            pltpu.VMEM((2, experts, part, LANES), BF16),
            pltpu.VMEM((2, experts, part, LANES), BF16),
            dma((5,)),
            dma((2, experts)),
            dma((2, experts)),
            dma((2, 3, experts)),
            dma((2, 3, experts)),
            dma((2,)),
            dma((2,)),
            dma((2, 2)),
            dma((2, 2)),
            dma((2, experts)),
            dma((2, experts)),
            dma((2, experts)),
            dma((2, experts)),
        ],
        compiler_params=pltpu.CompilerParams(
            collective_id=0, has_side_effects=True, vmem_limit_bytes=60 << 20
        ),
        cost_estimate=pl.CostEstimate(
            flops=16 * rows * width * units,
            bytes_accessed=6 * width * units + 12 * tok_count * width,
            transcendentals=rows * units,
        ),
    )(
        tokens,
        cotangent,
        ids_turned,
        gates.T,
        jnp.swapaxes(w_gate, 1, 2),
        jnp.swapaxes(w_up, 1, 2),
        w_down,
    )
    mixed_out, token_grad, gate_grad, down_grad = pl.pallas_call(
        functools.partial(combine_kernel, experts, capacity),
        out_shape=(
            jax.ShapeDtypeStruct((tok_count, width), BF16),
            jax.ShapeDtypeStruct((tok_count, width), BF16),
            jax.ShapeDtypeStruct(ids_turned.shape, F32),
            jax.ShapeDtypeStruct((1, units, width // 2), BF16),
        ),
        in_specs=[vmem] * 6,
        out_specs=(vmem,) * 4,
        scratch_shapes=[
            pltpu.VMEM((slots * pieces, LANES), F32),
            pltpu.VMEM((slots * pieces, LANES), F32),
        ],
        compiler_params=pltpu.CompilerParams(vmem_limit_bytes=60 << 20),
        cost_estimate=pl.CostEstimate(
            flops=8 * slots * width * tok_count,
            bytes_accessed=8 * tok_count * width,
            transcendentals=0,
        ),
    )(returned, pick, pick_gate, slot_cot, ids_turned, down)
    return mixed_out, token_grad, gate_grad.T, down_grad


def solution(mesh):
    rows = P(("pipe", "expert"), None)
    return jax.shard_map(
        functools.partial(body, mesh.shape["pipe"], mesh.shape["expert"]),
        mesh=mesh,
        in_specs=(
            rows,
            rows,
            rows,
            rows,
            P("pipe", None, "expert"),
            P("pipe", None, "expert"),
            P("pipe", "expert", None),
        ),
        out_specs=(rows, rows, rows, P("pipe", "expert", None)),
        check_vma=False,
    )
```

time: 42.3 us -> 31.8 us (0.75)
  local copies, waits for them, and re-layouts: 13.4 us -> 0 us
  Pallas kernels: 27.8 us -> 30.9 us
    unnamed x23 -> x0, local copies, waits for them, and re-layouts: 11.9 us -> none
    pallas_call x1 -> x2, Pallas kernels: 27.8 us -> 30.9 us  [the longest x1 27.9 us: body(): pl.pallas_call(functools.partial(moe_kernel, sections, devices, capacity)...]
    pallas_call x1 -> x0, local copies, waits for them, and re-layouts: 1.5 us -> none  [body(): pl.pallas_call(functools.partial(kernel, sections, devices, capacity), ou...]
where the time goes in v2:
time: 31.8 us; the launch traced here: 31.5 us
  Pallas kernels  30.9 us (97%)
  between operations  0.64 us (2%)
    pallas_call x1, Pallas kernels, body(): pl.pallas_call(functools.partial(moe_kernel, sections, devices, capacity)...  27.9 us
    pallas_call x1, Pallas kernels, body(): pl.pallas_call(functools.partial(combine_kernel, experts, capacity), out_...  3.02 us

profile of v2, /device:TPU:0, one launch (start us, length us, event | category | flops | bytes accessed | tf_op | source)
XLA Modules:
  0.0 31.5 jit_solution(9243107706583136533)
XLA Ops:
  0.6 27.9 %shard_map.102 = (bf16[2,4,80,128]{3,2,1,0:T(8,128)(2,1)}, f32[32,128]{1,0:T(8,128)}, f32[32,128]{1,0:T(8,128)}, f32[32,2048]{1,0:T(8,128)}, bf16[1,192,1024]{2,1,0:T(8,128)(2,1)}) custom-call(bf16[128,2048]{1,0:T(8,128)(2,1)} %tokens_hbm.1, bf16[128,2048]{1,0:T(8,128)(2,1)} %cot_hbm.1, s32[8,128]{1,0:T(8,128)} %bitcast.7, f32[8,128]{1,0:T(8,128)} %bitcast.9, ...), custom_call_target="tpu_custom_call" | custom-call | flops 503316480 | bytes 5505024 | tf_op jit(solution)/shard_map/pallas_call | solution.py:443
  28.5 3.0 %shard_map.103 = (bf16[128,2048]{1,0:T(8,128)(2,1)}, bf16[128,2048]{1,0:T(8,128)(2,1)}, f32[8,128]{1,0:T(8,128)}, bf16[1,192,1024]{2,1,0:T(8,128)(2,1)}) custom-call(bf16[2,4,80,128]{3,2,1,0:T(8,128)(2,1)} %get-tuple-element.13.returned_ref, f32[32,128]{1,0:T(8,128)} %get-tuple-element.14.pick_ref, f32[32,128]{1,0:T(8,128)} %get-tuple-element.15.pick_gate_ref, ...), custom_call_target="tpu_custom_call" | custom-call | flops 67108864 | bytes 2097152 | tf_op jit(solution)/shard_map/pallas_call | solution.py:506

commit v3 on v2

--- a/solution.py
+++ b/solution.py
@@ -35,11 +35,9 @@
     gate_hbm,
     up_hbm,
     down_hbm,
-    returned_ref,
-    pick_ref,
-    pick_gate_ref,
-    slot_cot_ref,
-    down_grad_ref,
+    returned_hbm,
+    slot_hbm,
+    down_grad_hbm,
     tokens,
     cot,
     w_gate,
@@ -60,11 +58,16 @@
     from_x,
     to_owner,
     returned,
+    slot_info,
+    down_grad,
     load_sem,
+    store_sem,
     z_send,
     z_recv,
     f_send,
     f_recv,
+    s_send,
+    s_recv,
     p_send,
     p_recv,
     a_send,
@@ -79,7 +82,7 @@
     pieces = width // LANES
     half = width // 2
     part = capacity * pieces
-    slots = slot_cot_ref.shape[0]
+    slots = slot_info.shape[0]
     row_count = devices * capacity
     section = lax.axis_index("pipe")
     me = lax.axis_index("expert")
@@ -104,6 +107,7 @@
         )
 
     outgoing = []
+    stores = []
 
     def push(*args):
         copy = remote(*args)
@@ -123,8 +127,8 @@
             ]
         )
     ]
-    for load in loads:
-        load.start()
+    loads[0].start()
+    loads[1].start()
     barrier = pltpu.get_barrier_semaphore()
     for d in range(1, experts):
         pl.semaphore_signal(
@@ -164,7 +168,6 @@
     order = range(experts)
     far_first = range(experts - 1, 0, -1)
     spots = {
-        "own": g,
         "core": x * 2 + (1 - core),
         "across": (1 - x) * 2 + core,
         "far": (1 - x) * 2 + (1 - core),
@@ -173,52 +176,53 @@
     def dispatch(kind, scratch):
         for e in range(experts):
             sent[kind, e] = scratch[e * part : (e + 1) * part].astype(BF16)
-        held[kind, 0, g] = sent[kind, w]
+        held[kind, g, 0] = sent[kind, w]
 
     def send_z(kind):
         for d in far_first:
             to = lax.rem(w + d, experts)
             push(
                 sent.at[kind, to],
-                held.at[kind, d, g],
+                held.at[kind, g, d],
                 z_send.at[kind, d],
                 z_recv.at[kind, d],
                 section,
                 owner(to),
             )
 
-    def arrive(kind, hop, d, spot):
-        block = held.at[kind, d, spots[spot]]
-        if hop == 3:
-            pair = (z_send.at[kind, d], z_recv.at[kind, d])
-        else:
-            pair = (f_send.at[kind, hop, d], f_recv.at[kind, hop, d])
-        remote(block, block, *pair, section, sibling).wait_recv()
-
-    def forward(kind, hop, d, spot, to):
-        block = held.at[kind, d, spots[spot]]
-        push(block, block, f_send.at[kind, hop, d], f_recv.at[kind, hop, d], section, to)
+    def to_across(kind, d):
+        block = held.at[kind, g, d]
+        push(block, block, f_send.at[kind, d], f_recv.at[kind, d], section, across)
 
     def spread(kind):
-        for d in order:
-            if d:
-                arrive(kind, 3, d, "own")
-            forward(kind, 0, d, "own", across)
-            forward(kind, 1, d, "own", sibling)
+        for d in range(1, experts):
+            block = held.at[kind, g, d]
+            remote(
+                block, block, z_send.at[kind, d], z_recv.at[kind, d], section, sibling
+            ).wait_recv()
+            to_across(kind, d)
+        block = held.at[kind, g]
+        push(block, block, s_send.at[kind, 0], s_recv.at[kind, 0], section, sibling)
 
     def pass_on(kind):
         for d in order:
-            arrive(kind, 0, d, "across")
-            forward(kind, 2, d, "across", sibling)
+            block = held.at[kind, spots["across"], d]
+            remote(
+                block, block, f_send.at[kind, d], f_recv.at[kind, d], section, across
+            ).wait_recv()
+        block = held.at[kind, spots["across"]]
+        push(block, block, s_send.at[kind, 1], s_recv.at[kind, 1], section, sibling)
 
     def collect(kind, scratch, rows):
-        for d in order:
-            arrive(kind, 1, d, "core")
-            arrive(kind, 2, d, "far")
+        for n, spot in enumerate(("core", "far")):
+            block = held.at[kind, spots[spot]]
+            remote(
+                block, block, s_send.at[kind, n], s_recv.at[kind, n], section, sibling
+            ).wait_recv()
         for d in order:
             for q in range(WS):
                 at = (d * WS + q) * part
-                scratch[at : at + part] = held[kind, d, q].astype(F32)
+                scratch[at : at + part] = held[kind, q, d].astype(F32)
         for j in range(pieces):
             rows[:, j * LANES : (j + 1) * LANES] = scratch[
                 pl.ds(j, row_count, stride=pieces), :
@@ -278,13 +282,18 @@
                 + from_x[kind, d].astype(F32)
             ).astype(BF16)
             if d == 0:
-                returned[kind, w] = total
+                returned[kind] = total
+                local = pltpu.make_async_copy(
+                    returned.at[kind], returned_hbm.at[kind, w], store_sem.at[1 + kind]
+                )
+                local.start()
+                stores.append(local)
             else:
                 to_owner[kind, d] = total
                 returns.append(
                     push(
                         to_owner.at[kind, d],
-                        returned.at[kind, w],
+                        returned_hbm.at[kind, w],
                         c_send.at[kind, d],
                         c_recv.at[kind, d],
                         section,
@@ -298,15 +307,21 @@
     dispatch(0, wide_a)
     pl.semaphore_wait(barrier, experts + 2)
     send_z(0)
+    to_across(0, 0)
+    for load in loads[2:]:
+        load.start()
     loads[1].wait()
     cot_rows = dot(pick_rows, cot[...])
     to_wire(wide_b, slot_gate * cot_rows, slots)
     dispatch(1, wide_b)
     send_z(1)
+    to_across(1, 0)
+    slot_info[:, :width] = cot_rows
+    slot_info[:, width : width + tok_count] = pick
+    slot_info[:, width + tok_count :] = pick_gate
+    slot_store = pltpu.make_async_copy(slot_info, slot_hbm, store_sem.at[0])
+    slot_store.start()
     spread(0)
-    slot_cot_ref[...] = cot_rows
-    pick_ref[...] = pick
-    pick_gate_ref[...] = pick_gate
     spread(1)
     pass_on(0)
     loads[2].wait()
@@ -357,12 +372,15 @@
     for copy in mirrored:
         copy.wait_recv()
     down_other = dot(hidden_other[...], scaled_other[...], ((0,), (0,)))
-    down_grad_ref[0] = (
+    down_grad[0] = (
         down_own.astype(F32) + down_other.astype(BF16).astype(F32)
     ).astype(BF16)
+    down_store = pltpu.make_async_copy(down_grad, down_grad_hbm, store_sem.at[3])
+    down_store.start()
+    for store in stores + [slot_store, down_store]:
+        store.wait()
     for copy in returns:
         copy.wait_recv()
-    returned_ref[...] = returned[...]
     for copy in outgoing:
         copy.wait_send()
 
@@ -370,33 +388,50 @@
 def combine_kernel(
     experts,
     capacity,
-    returned_ref,
-    pick_ref,
-    pick_gate_ref,
-    slot_cot_ref,
+    returned_hbm,
+    slot_hbm,
     ids_ref,
-    down_ref,
-    mixed_ref,
-    token_ref,
+    down_hbm,
+    mixed_hbm,
+    token_hbm,
     gate_grad_ref,
-    down_grad_ref,
+    down_grad_hbm,
+    returned,
+    slot_info,
+    down,
+    mixed,
+    token,
     wide_a,
     wide_b,
+    load_sem,
+    down_sem,
+    mixed_sem,
+    token_sem,
 ):
-    slots, width = slot_cot_ref.shape
+    slots = slot_info.shape[0]
+    tok_count, width = mixed.shape
     pieces = width // LANES
     part = capacity * pieces
-    down_grad_ref[...] = down_ref[...]
+    loads = [
+        pltpu.make_async_copy(returned_hbm, returned, load_sem.at[0]),
+        pltpu.make_async_copy(slot_hbm, slot_info, load_sem.at[1]),
+        pltpu.make_async_copy(down_hbm, down, load_sem.at[2]),
+    ]
+    for load in loads:
+        load.start()
+    named = named_slots(ids_ref[...], slots, experts, capacity)
+    loads[0].wait()
     for e in range(experts):
-        wide_a[e * part : (e + 1) * part] = returned_ref[0, e].astype(F32)
-        wide_b[e * part : (e + 1) * part] = returned_ref[1, e].astype(F32)
+        wide_a[e * part : (e + 1) * part] = returned[0, e].astype(F32)
+        wide_b[e * part : (e + 1) * part] = returned[1, e].astype(F32)
     if slots > experts * capacity:
         rest = slice(experts * part, slots * pieces)
         zero = jnp.zeros((slots * pieces - experts * part, LANES), F32)
         wide_a[rest] = zero
         wide_b[rest] = zero
-    pick = pick_ref[...]
-    pick_gate = pick_gate_ref[...]
+    loads[1].wait()
+    pick = slot_info[:, width : width + tok_count]
+    pick_gate = slot_info[:, width + tok_count :]
     turned = pick_gate.T
     high = turned.astype(BF16)
     left = turned - high.astype(F32)
@@ -404,27 +439,44 @@
     low = (left - mid.astype(F32)).astype(BF16)
     narrow_pick = pick.T.astype(BF16)
     value = jnp.zeros((slots, LANES), F32)
-    outs = []
-    grads = []
-    for j in range(pieces):
-        cols = slice(j * LANES, (j + 1) * LANES)
-        out = wide_a[pl.ds(j, slots, stride=pieces), :]
-        value += slot_cot_ref[:, cols] * out
-        outs.append(out.astype(BF16))
-        grads.append(wide_b[pl.ds(j, slots, stride=pieces), :].astype(BF16))
-    for j in range(0, pieces, 4):
-        cols = slice(j * LANES, (j + 4) * LANES)
-        out = jnp.concatenate(outs[j : j + 4], axis=1)
-        grad = jnp.concatenate(grads[j : j + 4], axis=1)
-        mixed_ref[:, cols] = (dot(low, out) + dot(mid, out) + dot(high, out)).astype(
-            BF16
-        )
-        token_ref[:, cols] = dot(narrow_pick, grad).astype(BF16)
+    stores = []
+
+    def write(src, dst, sem):
+        store = pltpu.make_async_copy(src, dst, sem)
+        store.start()
+        stores.append(store)
+
+    span = 4 if pieces % 4 == 0 else 1
+    for n, first in enumerate(range(0, pieces, span)):
+        cols = slice(first * LANES, (first + span) * LANES)
+        grads = [
+            wide_b[pl.ds(j, slots, stride=pieces), :].astype(BF16)
+            for j in range(first, first + span)
+        ]
+        grad = jnp.concatenate(grads, axis=1)
+        token[:, cols] = dot(narrow_pick, grad).astype(BF16)
+        write(token.at[:, cols], token_hbm.at[:, cols], token_sem.at[n])
+    loads[2].wait()
+    write(down, down_grad_hbm, down_sem)
+    for n, first in enumerate(range(0, pieces, span)):
+        cols = slice(first * LANES, (first + span) * LANES)
+        outs = [
+            wide_a[pl.ds(j, slots, stride=pieces), :]
+            for j in range(first, first + span)
+        ]
+        for j, out in enumerate(outs):
+            at = (first + j) * LANES
+            value += slot_info[:, at : at + LANES] * out
+        out = jnp.concatenate([out.astype(BF16) for out in outs], axis=1)
+        mixed[:, cols] = (dot(low, out) + dot(mid, out) + dot(high, out)).astype(BF16)
+        write(mixed.at[:, cols], mixed_hbm.at[:, cols], mixed_sem.at[n])
     spread = pick * jnp.sum(value, axis=1, keepdims=True)
-    for k, here in enumerate(named_slots(ids_ref[...], slots, experts, capacity)):
+    for k, here in enumerate(named):
         gate_grad_ref[k : k + 1, :] = jnp.sum(
             jnp.where(here, spread, 0.0), axis=0, keepdims=True
         )
+    for store in stores:
+        store.wait()
 
 
 def body(sections, devices, tokens, cotangent, expert_ids, gates, w_gate, w_up, w_down):
@@ -437,20 +489,18 @@
     slots = -(-experts * capacity // 16) * 16
     rows = devices * capacity
     dma = pltpu.SemaphoreType.DMA
-    far = pl.BlockSpec(memory_space=pltpu.HBM)
+    anywhere = pl.BlockSpec(memory_space=pl.ANY)
     vmem = pl.BlockSpec(memory_space=pltpu.VMEM)
     ids_turned = expert_ids.T
-    returned, pick, pick_gate, slot_cot, down = pl.pallas_call(
+    returned, slot_info, down = pl.pallas_call(
         functools.partial(moe_kernel, sections, devices, capacity),
         out_shape=(
             jax.ShapeDtypeStruct((2, experts, part, LANES), BF16),
-            jax.ShapeDtypeStruct((slots, tok_count), F32),
-            jax.ShapeDtypeStruct((slots, tok_count), F32),
-            jax.ShapeDtypeStruct((slots, width), F32),
+            jax.ShapeDtypeStruct((slots, width + 2 * tok_count), F32),
             jax.ShapeDtypeStruct((1, units, width // 2), BF16),
         ),
-        in_specs=[far, far, vmem, vmem, far, far, far],
-        out_specs=(vmem,) * 5,
+        in_specs=[anywhere, anywhere, vmem, vmem, anywhere, anywhere, anywhere],
+        out_specs=(anywhere,) * 3,
         scratch_shapes=[
             pltpu.VMEM((tok_count, width), BF16),
             pltpu.VMEM((tok_count, width), BF16),
@@ -460,7 +510,7 @@
             pltpu.VMEM((rows * pieces, LANES), F32),
             pltpu.VMEM((rows * pieces, LANES), F32),
             pltpu.VMEM((2, experts, part, LANES), BF16),
-            pltpu.VMEM((2, experts, WS, part, LANES), BF16),
+            pltpu.VMEM((2, WS, experts, part, LANES), BF16),
             pltpu.VMEM((rows, width), BF16),
             pltpu.VMEM((rows, width), BF16),
             pltpu.VMEM((rows, units), BF16),
@@ -471,12 +521,17 @@
             pltpu.VMEM((2, experts, part, LANES), BF16),
             pltpu.VMEM((2, experts, part, LANES), BF16),
             pltpu.VMEM((2, experts, part, LANES), BF16),
-            pltpu.VMEM((2, experts, part, LANES), BF16),
+            pltpu.VMEM((2, part, LANES), BF16),
+            pltpu.VMEM((slots, width + 2 * tok_count), F32),
+            pltpu.VMEM((1, units, width // 2), BF16),
             dma((5,)),
-            dma((2, experts)),
-            dma((2, experts)),
-            dma((2, 3, experts)),
-            dma((2, 3, experts)),
+            dma((4,)),
+            dma((2, experts)),
+            dma((2, experts)),
+            dma((2, experts)),
+            dma((2, experts)),
+            dma((2, 2)),
+            dma((2, 2)),
             dma((2,)),
             dma((2,)),
             dma((2, 2)),
@@ -511,11 +566,20 @@
             jax.ShapeDtypeStruct(ids_turned.shape, F32),
             jax.ShapeDtypeStruct((1, units, width // 2), BF16),
         ),
-        in_specs=[vmem] * 6,
-        out_specs=(vmem,) * 4,
+        in_specs=[anywhere, anywhere, vmem, anywhere],
+        out_specs=(anywhere, anywhere, vmem, anywhere),
         scratch_shapes=[
+            pltpu.VMEM((2, experts, part, LANES), BF16),
+            pltpu.VMEM((slots, width + 2 * tok_count), F32),
+            pltpu.VMEM((1, units, width // 2), BF16),
+            pltpu.VMEM((tok_count, width), BF16),
+            pltpu.VMEM((tok_count, width), BF16),
             pltpu.VMEM((slots * pieces, LANES), F32),
             pltpu.VMEM((slots * pieces, LANES), F32),
+            dma((3,)),
+            dma(()),
+            dma((pieces,)),
+            dma((pieces,)),
         ],
         compiler_params=pltpu.CompilerParams(vmem_limit_bytes=60 << 20),
         cost_estimate=pl.CostEstimate(
@@ -523,7 +587,7 @@
             bytes_accessed=8 * tok_count * width,
             transcendentals=0,
         ),
-    )(returned, pick, pick_gate, slot_cot, ids_turned, down)
+    )(returned, slot_info, ids_turned, down)
     return mixed_out, token_grad, gate_grad.T, down_grad
 
 

time: 31.8 us -> 32.1 us (level)
    pallas_call x1, Pallas kernels: 3.02 us -> 4.21 us  [body(): pl.pallas_call(functools.partial(combine_kernel, experts, capacity), out_...]
    pallas_call x1, Pallas kernels: 27.9 us -> 27 us  [body(): pl.pallas_call(functools.partial(moe_kernel, sections, devices, capacity)...]
where the time goes in v3:
time: 32.1 us; the launch traced here: 31.8 us
  Pallas kernels  31.2 us (97%)
  between operations  0.64 us (2%)
    pallas_call x1, Pallas kernels, body(): pl.pallas_call(functools.partial(moe_kernel, sections, devices, capacity)...  27 us
    pallas_call x1, Pallas kernels, body(): pl.pallas_call(functools.partial(combine_kernel, experts, capacity), out_...  4.21 us

profile of v3, /device:TPU:0, one launch (start us, length us, event | category | flops | bytes accessed | tf_op | source)
XLA Modules:
  0.0 31.8 jit_solution(16905189688312866399)
XLA Ops:
  0.6 27.0 %shard_map.102 = (bf16[2,4,80,128]{3,2,1,0:T(8,128)(2,1)}, f32[32,2304]{1,0:T(8,128)}, bf16[1,192,1024]{2,1,0:T(8,128)(2,1)}) custom-call(bf16[128,2048]{1,0:T(8,128)(2,1)} %tokens_hbm.1, bf16[128,2048]{1,0:T(8,128)(2,1)} %cot_hbm.1, s32[8,128]{1,0:T(8,128)} %bitcast.7, f32[8,128]{1,0:T(8,128)} %bitcast.9, bf16[1,192,2048]{2,1,0:T(8,128)(2,1)} %bitcast.5, ...), custom_call_target="tpu_custom_call" | custom-call | flops 503316480 | bytes 5505024 | tf_op jit(solution)/shard_map/pallas_call | solution.py:495
  27.6 4.2 %shard_map.103 = (bf16[128,2048]{1,0:T(8,128)(2,1)}, bf16[128,2048]{1,0:T(8,128)(2,1)}, f32[8,128]{1,0:T(8,128)}, bf16[1,192,1024]{2,1,0:T(8,128)(2,1)}) custom-call(bf16[2,4,80,128]{3,2,1,0:T(8,128)(2,1)} %get-tuple-element.11.returned_hbm, f32[32,2304]{1,0:T(8,128)} %get-tuple-element.12.slot_hbm, s32[8,128]{1,0:T(8,128)} %bitcast.8, ...), custom_call_target="tpu_custom_call" | custom-call | flops 67108864 | bytes 2097152 | tf_op jit(solution)/shard_map/pallas_call | solution.py:561

commit v4 on v3

--- a/solution.py
+++ b/solution.py
@@ -40,8 +40,7 @@
     down_grad_hbm,
     tokens,
     cot,
-    w_gate,
-    w_up,
+    w_both,
     w_down,
     wide_a,
     wide_b,
@@ -81,6 +80,7 @@
     tok_count, width = tokens.shape
     pieces = width // LANES
     half = width // 2
+    units = w_down.shape[0]
     part = capacity * pieces
     slots = slot_info.shape[0]
     row_count = devices * capacity
@@ -121,8 +121,8 @@
             [
                 (tokens_hbm, tokens),
                 (cot_hbm, cot),
-                (gate_hbm.at[0], w_gate),
-                (up_hbm.at[0], w_up),
+                (gate_hbm.at[0], w_both.at[:units]),
+                (up_hbm.at[0], w_both.at[units:]),
                 (down_hbm.at[0], w_down),
             ]
         )
@@ -164,6 +164,15 @@
             scratch[pl.ds(j, count, stride=pieces), :] = values[
                 :, j * LANES : (j + 1) * LANES
             ]
+
+    def product_to_wire(scratch, left, right):
+        span = 4 if pieces % 4 == 0 else 1
+        for first in range(0, pieces, span):
+            values = dot(left, right[:, first * LANES : (first + span) * LANES])
+            for j in range(span):
+                scratch[pl.ds(first + j, row_count, stride=pieces), :] = values[
+                    :, j * LANES : (j + 1) * LANES
+                ]
 
     order = range(experts)
     far_first = range(experts - 1, 0, -1)
@@ -328,15 +337,16 @@
     loads[3].wait()
     loads[4].wait()
     collect(0, wide_a, rows_in)
-    gate_pre = dot(rows_in[...], w_gate[...], transposed)
-    up_pre = dot(rows_in[...], w_up[...], transposed)
+    both_pre = dot(rows_in[...], w_both[...], transposed)
+    gate_pre = both_pre[:, :units]
+    up_pre = both_pre[:, units:]
     sigmoid = jax.nn.sigmoid(gate_pre)
     activated = gate_pre * sigmoid
     slope = sigmoid * (1.0 + gate_pre * (1.0 - sigmoid))
     hidden = (activated * up_pre).astype(BF16)
     hidden_own[...] = hidden
     pass_on(1)
-    to_wire(wide_a, dot(hidden, w_down[...]), row_count)
+    product_to_wire(wide_a, hidden, w_down)
     out_cores = fold_cores(0, wide_a)
     mirrored = [push(hidden_own, hidden_other, p_send.at[1], p_recv.at[1], mirror, me)]
 
@@ -358,11 +368,7 @@
     hidden_grad = dot(rows_scaled[...], w_down[...], transposed)
     grad_gate = (hidden_grad * up_pre * slope).astype(BF16)
     grad_up = (hidden_grad * activated).astype(BF16)
-    to_wire(
-        wide_b,
-        dot(grad_gate, w_gate[...]) + dot(grad_up, w_up[...]),
-        row_count,
-    )
+    product_to_wire(wide_b, jnp.concatenate([grad_gate, grad_up], axis=1), w_both)
     grad_cores = fold_cores(1, wide_b)
     returns = give_back(0, out_crossing)
     grad_crossing = fold_x(1, grad_cores)
@@ -388,95 +394,58 @@
 def combine_kernel(
     experts,
     capacity,
-    returned_hbm,
-    slot_hbm,
+    returned_ref,
+    slot_ref,
     ids_ref,
-    down_hbm,
-    mixed_hbm,
-    token_hbm,
+    down_ref,
+    mixed_ref,
+    token_ref,
     gate_grad_ref,
-    down_grad_hbm,
-    returned,
-    slot_info,
-    down,
-    mixed,
-    token,
+    down_grad_ref,
     wide_a,
     wide_b,
-    load_sem,
-    down_sem,
-    mixed_sem,
-    token_sem,
 ):
-    slots = slot_info.shape[0]
-    tok_count, width = mixed.shape
+    slots = slot_ref.shape[0]
+    tok_count, width = mixed_ref.shape
     pieces = width // LANES
     part = capacity * pieces
-    loads = [
-        pltpu.make_async_copy(returned_hbm, returned, load_sem.at[0]),
-        pltpu.make_async_copy(slot_hbm, slot_info, load_sem.at[1]),
-        pltpu.make_async_copy(down_hbm, down, load_sem.at[2]),
-    ]
-    for load in loads:
-        load.start()
-    named = named_slots(ids_ref[...], slots, experts, capacity)
-    loads[0].wait()
+    down_grad_ref[...] = down_ref[...]
     for e in range(experts):
-        wide_a[e * part : (e + 1) * part] = returned[0, e].astype(F32)
-        wide_b[e * part : (e + 1) * part] = returned[1, e].astype(F32)
+        wide_a[e * part : (e + 1) * part] = returned_ref[0, e].astype(F32)
+        wide_b[e * part : (e + 1) * part] = returned_ref[1, e].astype(F32)
     if slots > experts * capacity:
         rest = slice(experts * part, slots * pieces)
         zero = jnp.zeros((slots * pieces - experts * part, LANES), F32)
         wide_a[rest] = zero
         wide_b[rest] = zero
-    loads[1].wait()
-    pick = slot_info[:, width : width + tok_count]
-    pick_gate = slot_info[:, width + tok_count :]
-    turned = pick_gate.T
-    high = turned.astype(BF16)
-    left = turned - high.astype(F32)
-    mid = left.astype(BF16)
-    low = (left - mid.astype(F32)).astype(BF16)
+    pick = slot_ref[:, width : width + tok_count]
+    pick_gate = slot_ref[:, width + tok_count :]
+    high = pick_gate.astype(BF16).astype(F32)
+    mid = (pick_gate - high).astype(BF16).astype(F32)
+    low = pick_gate - high - mid
+    terms = jnp.concatenate([low, mid, high], axis=0).T.astype(BF16)
     narrow_pick = pick.T.astype(BF16)
     value = jnp.zeros((slots, LANES), F32)
-    stores = []
-
-    def write(src, dst, sem):
-        store = pltpu.make_async_copy(src, dst, sem)
-        store.start()
-        stores.append(store)
-
     span = 4 if pieces % 4 == 0 else 1
-    for n, first in enumerate(range(0, pieces, span)):
+    for first in range(0, pieces, span):
         cols = slice(first * LANES, (first + span) * LANES)
-        grads = [
-            wide_b[pl.ds(j, slots, stride=pieces), :].astype(BF16)
-            for j in range(first, first + span)
-        ]
-        grad = jnp.concatenate(grads, axis=1)
-        token[:, cols] = dot(narrow_pick, grad).astype(BF16)
-        write(token.at[:, cols], token_hbm.at[:, cols], token_sem.at[n])
-    loads[2].wait()
-    write(down, down_grad_hbm, down_sem)
-    for n, first in enumerate(range(0, pieces, span)):
-        cols = slice(first * LANES, (first + span) * LANES)
-        outs = [
-            wide_a[pl.ds(j, slots, stride=pieces), :]
-            for j in range(first, first + span)
-        ]
-        for j, out in enumerate(outs):
-            at = (first + j) * LANES
-            value += slot_info[:, at : at + LANES] * out
-        out = jnp.concatenate([out.astype(BF16) for out in outs], axis=1)
-        mixed[:, cols] = (dot(low, out) + dot(mid, out) + dot(high, out)).astype(BF16)
-        write(mixed.at[:, cols], mixed_hbm.at[:, cols], mixed_sem.at[n])
+        outs = []
+        grads = []
+        for j in range(first, first + span):
+            out = wide_a[pl.ds(j, slots, stride=pieces), :]
+            value += slot_ref[:, j * LANES : (j + 1) * LANES] * out
+            outs.append(out.astype(BF16))
+            grads.append(wide_b[pl.ds(j, slots, stride=pieces), :].astype(BF16))
+        out = jnp.concatenate(outs, axis=1)
+        mixed_ref[:, cols] = dot(terms, jnp.concatenate([out] * 3, axis=0)).astype(BF16)
+        token_ref[:, cols] = dot(narrow_pick, jnp.concatenate(grads, axis=1)).astype(
+            BF16
+        )
     spread = pick * jnp.sum(value, axis=1, keepdims=True)
-    for k, here in enumerate(named):
+    for k, here in enumerate(named_slots(ids_ref[...], slots, experts, capacity)):
         gate_grad_ref[k : k + 1, :] = jnp.sum(
             jnp.where(here, spread, 0.0), axis=0, keepdims=True
         )
-    for store in stores:
-        store.wait()
 
 
 def body(sections, devices, tokens, cotangent, expert_ids, gates, w_gate, w_up, w_down):
@@ -504,8 +473,7 @@
         scratch_shapes=[
             pltpu.VMEM((tok_count, width), BF16),
             pltpu.VMEM((tok_count, width), BF16),
-            pltpu.VMEM((units, width), BF16),
-            pltpu.VMEM((units, width), BF16),
+            pltpu.VMEM((2 * units, width), BF16),
             pltpu.VMEM((units, width), BF16),
             pltpu.VMEM((rows * pieces, LANES), F32),
             pltpu.VMEM((rows * pieces, LANES), F32),
@@ -566,20 +534,11 @@
             jax.ShapeDtypeStruct(ids_turned.shape, F32),
             jax.ShapeDtypeStruct((1, units, width // 2), BF16),
         ),
-        in_specs=[anywhere, anywhere, vmem, anywhere],
-        out_specs=(anywhere, anywhere, vmem, anywhere),
+        in_specs=[vmem] * 4,
+        out_specs=(vmem,) * 4,
         scratch_shapes=[
-            pltpu.VMEM((2, experts, part, LANES), BF16),
-            pltpu.VMEM((slots, width + 2 * tok_count), F32),
-            pltpu.VMEM((1, units, width // 2), BF16),
-            pltpu.VMEM((tok_count, width), BF16),
-            pltpu.VMEM((tok_count, width), BF16),
             pltpu.VMEM((slots * pieces, LANES), F32),
             pltpu.VMEM((slots * pieces, LANES), F32),
-            dma((3,)),
-            dma(()),
-            dma((pieces,)),
-            dma((pieces,)),
         ],
         compiler_params=pltpu.CompilerParams(vmem_limit_bytes=60 << 20),
         cost_estimate=pl.CostEstimate(

time: 32.1 us -> 30.8 us (0.960)
  Pallas kernels: 31.2 us -> 29.9 us
    pallas_call x1, Pallas kernels: 4.21 us -> 2.74 us  [body(): pl.pallas_call(functools.partial(combine_kernel, experts, capacity), out_...]
where the time goes in v4:
time: 30.8 us; the launch traced here: 30.6 us
  Pallas kernels  29.9 us (97%)
  between operations  0.64 us (2%)
    pallas_call x1, Pallas kernels, body(): pl.pallas_call(functools.partial(moe_kernel, sections, devices, capacity)...  27.2 us
    pallas_call x1, Pallas kernels, body(): pl.pallas_call(functools.partial(combine_kernel, experts, capacity), out_...  2.74 us

profile of v4, /device:TPU:0, one launch (start us, length us, event | category | flops | bytes accessed | tf_op | source)
XLA Modules:
  0.0 30.6 jit_solution(7808183025654634436)
XLA Ops:
  0.6 27.2 %shard_map.102 = (bf16[2,4,80,128]{3,2,1,0:T(8,128)(2,1)}, f32[32,2304]{1,0:T(8,128)}, bf16[1,192,1024]{2,1,0:T(8,128)(2,1)}) custom-call(bf16[128,2048]{1,0:T(8,128)(2,1)} %tokens_hbm.1, bf16[128,2048]{1,0:T(8,128)(2,1)} %cot_hbm.1, s32[8,128]{1,0:T(8,128)} %bitcast.7, f32[8,128]{1,0:T(8,128)} %bitcast.9, bf16[1,192,2048]{2,1,0:T(8,128)(2,1)} %bitcast.5, ...), custom_call_target="tpu_custom_call" | custom-call | flops 503316480 | bytes 5505024 | tf_op jit(solution)/shard_map/pallas_call | solution.py:464
  27.8 2.7 %shard_map.103 = (bf16[128,2048]{1,0:T(8,128)(2,1)}, bf16[128,2048]{1,0:T(8,128)(2,1)}, f32[8,128]{1,0:T(8,128)}, bf16[1,192,1024]{2,1,0:T(8,128)(2,1)}) custom-call(bf16[2,4,80,128]{3,2,1,0:T(8,128)(2,1)} %get-tuple-element.11.returned_ref, f32[32,2304]{1,0:T(8,128)} %get-tuple-element.12.slot_ref, s32[8,128]{1,0:T(8,128)} %bitcast.8, ...), custom_call_target="tpu_custom_call" | custom-call | flops 67108864 | bytes 2097152 | tf_op jit(solution)/shard_map/pallas_call | solution.py:529

commit v5 on v4

--- a/solution.py
+++ b/solution.py
@@ -30,14 +30,16 @@
     capacity,
     tokens_hbm,
     cot_hbm,
-    ids_ref,
-    gates_ref,
+    ids_hbm,
+    gates_hbm,
     gate_hbm,
     up_hbm,
     down_hbm,
     returned_hbm,
     slot_hbm,
     down_grad_hbm,
+    ids_ref,
+    gates_ref,
     tokens,
     cot,
     w_both,
@@ -124,11 +126,13 @@
                 (gate_hbm.at[0], w_both.at[:units]),
                 (up_hbm.at[0], w_both.at[units:]),
                 (down_hbm.at[0], w_down),
+                (ids_hbm, ids_ref),
+                (gates_hbm, gates_ref),
             ]
         )
     ]
-    loads[0].start()
-    loads[1].start()
+    for i in (5, 6, 0, 1):
+        loads[i].start()
     barrier = pltpu.get_barrier_semaphore()
     for d in range(1, experts):
         pl.semaphore_signal(
@@ -140,6 +144,11 @@
     for target in ((section, sibling), (section, across), (mirror, me)):
         pl.semaphore_signal(barrier, inc=1, device_id=target, device_id_type=MESH)
 
+    row_no = lax.broadcasted_iota(jnp.int32, (tok_count, tok_count), 0)
+    col_no = lax.broadcasted_iota(jnp.int32, (tok_count, tok_count), 1)
+    before = jnp.where(row_no < col_no, 1.0, 0.0).astype(BF16)
+    loads[5].wait()
+    loads[6].wait()
     ids = ids_ref[...]
     gates = gates_ref[...]
     named = named_slots(ids, slots, experts, capacity)
@@ -148,9 +157,6 @@
     for k, here in enumerate(named):
         match += jnp.where(here, 1.0, 0.0)
         weight += jnp.where(here, gates[k : k + 1, :], 0.0)
-    row_no = lax.broadcasted_iota(jnp.int32, (tok_count, tok_count), 0)
-    col_no = lax.broadcasted_iota(jnp.int32, (tok_count, tok_count), 1)
-    before = jnp.where(row_no < col_no, 1.0, 0.0).astype(BF16)
     earlier = dot(match.astype(BF16), before)
     slot = lax.broadcasted_iota(jnp.int32, (slots, tok_count), 0)
     slot_rank = (slot % capacity).astype(F32)
@@ -204,7 +210,7 @@
         push(block, block, f_send.at[kind, d], f_recv.at[kind, d], section, across)
 
     def spread(kind):
-        for d in range(1, experts):
+        for d in far_first:
             block = held.at[kind, g, d]
             remote(
                 block, block, z_send.at[kind, d], z_recv.at[kind, d], section, sibling
@@ -214,7 +220,7 @@
         push(block, block, s_send.at[kind, 0], s_recv.at[kind, 0], section, sibling)
 
     def pass_on(kind):
-        for d in order:
+        for d in (0, *far_first):
             block = held.at[kind, spots["across"], d]
             remote(
                 block, block, f_send.at[kind, d], f_recv.at[kind, d], section, across
@@ -317,7 +323,7 @@
     pl.semaphore_wait(barrier, experts + 2)
     send_z(0)
     to_across(0, 0)
-    for load in loads[2:]:
+    for load in loads[2:5]:
         load.start()
     loads[1].wait()
     cot_rows = dot(pick_rows, cot[...])
@@ -468,9 +474,11 @@
             jax.ShapeDtypeStruct((slots, width + 2 * tok_count), F32),
             jax.ShapeDtypeStruct((1, units, width // 2), BF16),
         ),
-        in_specs=[anywhere, anywhere, vmem, vmem, anywhere, anywhere, anywhere],
+        in_specs=[anywhere] * 7,
         out_specs=(anywhere,) * 3,
         scratch_shapes=[
+            pltpu.VMEM(ids_turned.shape, jnp.int32),
+            pltpu.VMEM(ids_turned.shape, F32),
             pltpu.VMEM((tok_count, width), BF16),
             pltpu.VMEM((tok_count, width), BF16),
             pltpu.VMEM((2 * units, width), BF16),
@@ -492,7 +500,7 @@
             pltpu.VMEM((2, part, LANES), BF16),
             pltpu.VMEM((slots, width + 2 * tok_count), F32),
             pltpu.VMEM((1, units, width // 2), BF16),
-            dma((5,)),
+            dma((7,)),
             dma((4,)),
             dma((2, experts)),
             dma((2, experts)),

time: 30.8 us -> 30.4 us (0.987)
    pallas_call x1, Pallas kernels: 27.2 us -> 26.9 us  [body(): pl.pallas_call(functools.partial(moe_kernel, sections, devices, capacity)...]
where the time goes in v5:
time: 30.4 us; the launch traced here: 30.3 us
  Pallas kernels  29.6 us (97%)
  between operations  0.64 us (2%)
    pallas_call x1, Pallas kernels, body(): pl.pallas_call(functools.partial(moe_kernel, sections, devices, capacity)...  26.9 us
    pallas_call x1, Pallas kernels, body(): pl.pallas_call(functools.partial(combine_kernel, experts, capacity), out_...  2.74 us

profile of v5, /device:TPU:0, one launch (start us, length us, event | category | flops | bytes accessed | tf_op | source)
XLA Modules:
  0.0 30.3 jit_solution(9619216334184116475)
XLA Ops:
  0.6 26.9 %shard_map.102 = (bf16[2,4,80,128]{3,2,1,0:T(8,128)(2,1)}, f32[32,2304]{1,0:T(8,128)}, bf16[1,192,1024]{2,1,0:T(8,128)(2,1)}) custom-call(bf16[128,2048]{1,0:T(8,128)(2,1)} %tokens_hbm.1, bf16[128,2048]{1,0:T(8,128)(2,1)} %cot_hbm.1, s32[8,128]{1,0:T(8,128)} %bitcast.7, f32[8,128]{1,0:T(8,128)} %bitcast.9, bf16[1,192,2048]{2,1,0:T(8,128)(2,1)} %bitcast.5, ...), custom_call_target="tpu_custom_call" | custom-call | flops 503316480 | bytes 5505024 | tf_op jit(solution)/shard_map/pallas_call | solution.py:470
  27.5 2.7 %shard_map.103 = (bf16[128,2048]{1,0:T(8,128)(2,1)}, bf16[128,2048]{1,0:T(8,128)(2,1)}, f32[8,128]{1,0:T(8,128)}, bf16[1,192,1024]{2,1,0:T(8,128)(2,1)}) custom-call(bf16[2,4,80,128]{3,2,1,0:T(8,128)(2,1)} %get-tuple-element.11.returned_ref, f32[32,2304]{1,0:T(8,128)} %get-tuple-element.12.slot_ref, s32[8,128]{1,0:T(8,128)} %bitcast.8, ...), custom_call_target="tpu_custom_call" | custom-call | flops 67108864 | bytes 2097152 | tf_op jit(solution)/shard_map/pallas_call | solution.py:537

commit v6 on v5

--- a/solution.py
+++ b/solution.py
@@ -378,9 +378,9 @@
     grad_cores = fold_cores(1, wide_b)
     returns = give_back(0, out_crossing)
     grad_crossing = fold_x(1, grad_cores)
+    returns += give_back(1, grad_crossing)
     down_own = dot(hidden_own[...], rows_scaled[:, own_cols], ((0,), (0,)))
     down_own = down_own.astype(BF16)
-    returns += give_back(1, grad_crossing)
     for copy in mirrored:
         copy.wait_recv()
     down_other = dot(hidden_other[...], scaled_other[...], ((0,), (0,)))

time: 30.4 us -> 30.4 us (level)
  no operation moved by 1% of the time
where the time goes in v6:
time: 30.4 us; the launch traced here: 30.3 us
  Pallas kernels  29.6 us (97%)
  between operations  0.64 us (2%)
    pallas_call x1, Pallas kernels, body(): pl.pallas_call(functools.partial(moe_kernel, sections, devices, capacity)...  26.9 us
    pallas_call x1, Pallas kernels, body(): pl.pallas_call(functools.partial(combine_kernel, experts, capacity), out_...  2.74 us

profile of v6, /device:TPU:0, one launch (start us, length us, event | category | flops | bytes accessed | tf_op | source)
XLA Modules:
  0.0 30.3 jit_solution(13674629522778340706)
XLA Ops:
  0.6 26.9 %shard_map.102 = (bf16[2,4,80,128]{3,2,1,0:T(8,128)(2,1)}, f32[32,2304]{1,0:T(8,128)}, bf16[1,192,1024]{2,1,0:T(8,128)(2,1)}) custom-call(bf16[128,2048]{1,0:T(8,128)(2,1)} %tokens_hbm.1, bf16[128,2048]{1,0:T(8,128)(2,1)} %cot_hbm.1, s32[8,128]{1,0:T(8,128)} %bitcast.7, f32[8,128]{1,0:T(8,128)} %bitcast.9, bf16[1,192,2048]{2,1,0:T(8,128)(2,1)} %bitcast.5, ...), custom_call_target="tpu_custom_call" | custom-call | flops 503316480 | bytes 5505024 | tf_op jit(solution)/shard_map/pallas_call | solution.py:470
  27.5 2.7 %shard_map.103 = (bf16[128,2048]{1,0:T(8,128)(2,1)}, bf16[128,2048]{1,0:T(8,128)(2,1)}, f32[8,128]{1,0:T(8,128)}, bf16[1,192,1024]{2,1,0:T(8,128)(2,1)}) custom-call(bf16[2,4,80,128]{3,2,1,0:T(8,128)(2,1)} %get-tuple-element.11.returned_ref, f32[32,2304]{1,0:T(8,128)} %get-tuple-element.12.slot_ref, s32[8,128]{1,0:T(8,128)} %bitcast.8, ...), custom_call_target="tpu_custom_call" | custom-call | flops 67108864 | bytes 2097152 | tf_op jit(solution)/shard_map/pallas_call | solution.py:537
